TPU v7x, 256 devices: a whole 4x4x8 slice. The times are simulated.
256 devices in a mesh: rows: 64 (over y, z_hi, x, core), heads: 4 (over z_lo).
Axes of the slice: x: 4, y: 4, z: 8 (z_hi: 2, z_lo: 4; z = z_hi * 4 + z_lo), core: 2. Of those that a mesh axis runs over, the one named last changes fastest.
Arguments:
- slab: bfloat16 [256, 1024, 128], P('rows'), may hold values from -6 to 6
- pair: bfloat16 [1024, 1024, 128], P('rows'), may hold values from -6 to 6
- pair_mask: int32 [256, 1024], P('rows'), may hold values from 0 to 1, as said below
- w_qkvg: bfloat16 [128, 4, 128], P(None, None, 'heads')
- w_out: bfloat16 [128, 128], P('heads'), may hold values from -0.5 to 0.5
- w_bias: bfloat16 [128, 4], replicated
- d_out: bfloat16 [256, 1024, 128], P('rows'), may hold values from -16 to 16
Outputs:
- d_slab: bfloat16 [256, 1024, 128], P('rows')
- d_pair: bfloat16 [1024, 1024, 128], P('rows', None, 'heads')
- d_wqkvg: float32 [128, 4, 128], P(None, None, 'heads')
- d_wout: float32 [128, 128], P('heads')
- d_wbias: float32 [128, 4], P(None, 'heads')
Inputs may be any that keep to these rules, and one draw needn't show every extreme that they name: pair_mask[i, k] is the product of two residue flags, of residue i and residue k; the 1024 residues form 4 chains of 256, each ending in a run of padded residues of length 0 to half the chain (128); the first residue of every chain is real.
All inputs are finite; a program needn't handle non-finite values.
Results may differ from a plain program's by a relative error of at most 0.017.
The roundings to bfloat16 on the way count: a program that leaves them out, or rounds other values in their place, can miss the bound.
Values may be sent and summed in bfloat16 or wider, within the bound.
A program may use at most 128 MiB of HBM per device.

v0:
```python
import math

import jax
import jax.numpy as jnp
from jax import lax
from jax.sharding import PartitionSpec as P


def norm_stats(tensor):
    full = tensor.astype(jnp.float32)
    center = full - jnp.mean(full, axis=-1, keepdims=True)
    recip = lax.rsqrt(jnp.mean(center * center, axis=-1, keepdims=True) + 1e-05)
    return (center * recip, recip)


def norm_back(normed, recip, grad):
    first = jnp.mean(grad, axis=-1, keepdims=True)
    second = jnp.mean(grad * normed, axis=-1, keepdims=True)
    return recip * (grad - first - normed * second)


def block_terms(query_block, datt_block, bias_block, key_vecs, values, keep_mask, scale):
    raw = (
        jnp.einsum("sjd,skd->sjk", query_block, key_vecs, preferred_element_type=jnp.float32)
        * scale
        + bias_block.astype(jnp.float32)[None]
    )
    logits = jnp.where(keep_mask[:, None, :], raw, -1000000000.0)
    top = jnp.max(logits, axis=-1, keepdims=True)
    expo = jnp.exp(logits - top)
    probs = expo / jnp.sum(expo, axis=-1, keepdims=True)
    probs_b = probs.astype(jnp.bfloat16)
    att_block = jnp.einsum("sjk,skd->sjd", probs_b, values, preferred_element_type=jnp.float32)
    d_probs = jnp.einsum("sjd,skd->sjk", datt_block, values, preferred_element_type=jnp.float32)
    d_logits = probs * (d_probs - jnp.sum(probs * d_probs, axis=-1, keepdims=True))
    d_logits = jnp.where(keep_mask[:, None, :], d_logits, 0.0)
    logits_b = d_logits.astype(jnp.bfloat16)
    dq_block = jnp.einsum("sjk,skd->sjd", logits_b, key_vecs, preferred_element_type=jnp.float32)
    dk_add = jnp.einsum("sjk,sjd->skd", logits_b, query_block, preferred_element_type=jnp.float32)
    dv_add = jnp.einsum("sjk,sjd->skd", probs_b, datt_block, preferred_element_type=jnp.float32)
    return (jnp.sum(d_logits, axis=0), att_block, dq_block, dk_add, dv_add)


def shards(slab, pair, pair_mask, w_qkvg, w_out, w_bias, d_out):
    width = slab.shape[2]
    head_size = w_out.shape[0]
    scale = 1.0 / head_size**0.5
    head_index = lax.axis_index("heads")
    normed_slab, slab_r = norm_stats(slab)
    x_slab = normed_slab.astype(jnp.bfloat16)
    proj = jnp.einsum("snc,cfd->snfd", x_slab, w_qkvg, preferred_element_type=jnp.float32)
    queries = proj[:, :, 0].astype(jnp.bfloat16)
    key_vecs = proj[:, :, 1].astype(jnp.bfloat16)
    values = proj[:, :, 2].astype(jnp.bfloat16)
    gate = jax.nn.sigmoid(proj[:, :, 3])
    normed_pair, pair_r = norm_stats(pair)
    x_pair = normed_pair.astype(jnp.bfloat16)
    bias_column = lax.dynamic_slice_in_dim(w_bias, head_index, 1, 1)
    bias_rows = jnp.einsum(
        "jkc,ch->jk", x_pair, bias_column, preferred_element_type=jnp.float32
    ).astype(jnp.bfloat16)
    d_o = jnp.einsum("snc,dc->snd", d_out, w_out, preferred_element_type=jnp.float32)
    d_att = (d_o * gate).astype(jnp.bfloat16)
    keep_mask = pair_mask == 1
    residues = pair_mask.shape[1]
    zero_plane = jnp.zeros((residues, residues), jnp.float32)
    zero_rows = jnp.zeros(queries.shape, jnp.float32)
    start_carry = (zero_plane, zero_rows, zero_rows, zero_rows, zero_rows)
    plane = lax.all_gather(bias_rows, "rows", axis=0, tiled=True)
    count = plane.shape[0]
    block = math.gcd(count, 128)

    def inner(step, state):
        d_bias, attended, d_query, d_key, d_value = state
        offset = step * block
        first = 0 + offset
        bias_block = lax.dynamic_slice_in_dim(plane, offset, block, 0)
        query_block = lax.dynamic_slice_in_dim(queries, first, block, 1)
        datt_block = lax.dynamic_slice_in_dim(d_att, first, block, 1)
        terms = block_terms(query_block, datt_block, bias_block, key_vecs, values, keep_mask, scale)
        d_bias = lax.dynamic_update_slice_in_dim(d_bias, terms[0], first, 0)
        attended = lax.dynamic_update_slice_in_dim(attended, terms[1], first, 1)
        d_query = lax.dynamic_update_slice_in_dim(d_query, terms[2], first, 1)
        return (d_bias, attended, d_query, d_key + terms[3], d_value + terms[4])

    bias_part, attended, dq_raw, dk_raw, dv_raw = lax.fori_loop(
        0, count // block, inner, start_carry
    )
    bias_mine = lax.psum_scatter(bias_part, "rows", scatter_dimension=0, tiled=True)
    gated = (gate * attended).astype(jnp.bfloat16)
    d_gate = (d_o * attended * gate * (1.0 - gate)).astype(jnp.bfloat16)
    d_queries = (dq_raw * scale).astype(jnp.bfloat16)
    d_keys = (dk_raw * scale).astype(jnp.bfloat16)
    d_values = dv_raw.astype(jnp.bfloat16)
    grads = jnp.stack([d_queries, d_keys, d_values, d_gate], axis=2)
    dw_head = jnp.einsum("snc,snfd->cfd", x_slab, grads, preferred_element_type=jnp.float32)
    dwout_head = jnp.einsum("snd,snc->dc", gated, d_out, preferred_element_type=jnp.float32)
    dx_part = jnp.einsum("snfd,cfd->snc", grads, w_qkvg, preferred_element_type=jnp.float32)
    d_xslab = lax.psum(dx_part.astype(jnp.bfloat16), "heads").astype(jnp.float32)
    d_slab = norm_back(normed_slab, slab_r, d_xslab).astype(jnp.bfloat16)
    dwbias_head = jnp.einsum(
        "jkc,jk->c", x_pair.astype(jnp.float32), bias_mine, precision=lax.Precision.HIGHEST
    )[:, None]
    quarter = width // lax.axis_size("heads")
    every_head = lax.all_gather(
        bias_mine[None].astype(jnp.bfloat16), "heads", axis=0, tiled=True
    ).astype(jnp.float32)
    d_xpair = jnp.einsum(
        "hjk,ch->jkc", every_head, w_bias.astype(jnp.float32), precision=lax.Precision.HIGHEST
    )
    whole_grad = norm_back(normed_pair, pair_r, d_xpair)
    d_pair = lax.dynamic_slice_in_dim(whole_grad, head_index * quarter, quarter, 2).astype(
        jnp.bfloat16
    )
    summed = lax.psum((dw_head, dwout_head, dwbias_head), "rows")
    return (d_slab, d_pair, summed[0], summed[1], summed[2])


def solution(mesh):
    placed = (
        P("rows", None, None),
        P("rows", None, None),
        P("rows", None),
        P(None, None, "heads"),
        P("heads", None),
        P(),
        P("rows", None, None),
    )
    return jax.shard_map(
        shards,
        mesh=mesh,
        in_specs=placed,
        out_specs=(
            P("rows", None, None),
            P("rows", None, "heads"),
            P(None, None, "heads"),
            P("heads", None),
            P(None, "heads"),
        ),
        check_vma=False,
    )
```

profile of v0, /device:TPU:1, one launch (start us, length us, event | category | flops | bytes accessed | tf_op | source)
XLA Modules:
  0.0 1527.6 jit_solution(5756361954979580653)
XLA Ops:
  7.2 6.5 copy.14
  13.7 3.3 convert_reduce_fusion
  18.4 3.4 fusion.77
  25.1 3.0 fusion.118
  31.0 78.7 %all-gather.3.cloned.1.call-done = bf16[1024,1024]{1,0:T(8,128)(2,1)} async-done(((bf16[16,1024]{1,0:T(8,128)(2,1)}), bf16[1024,1024]{1,0:T(8,128)(2,1)}) %all-gather.3.cloned.1.call-update) | async-done | bytes 2097168 | tf_op jit(solution)/shard_map/all_gather | solution.py:69
  113.9 222.5 %while.22 = (s32[]{:T(128)}, f32[1024,1024]{1,0:T(8,128)}, f32[4,1024,32]{1,2,0:T(8,128)}, f32[4,1024,32]{1,2,0:T(8,128)}, f32[4,1024,32]{1,2,0:T(8,128)}, /*ind...) while((s32[]{:T(128)}, f32[1024,1024]{1,0:T(8,128)}, ...), condition=%wide.region_9.0_spmd.clone, body=%wide.region_4.9_spmd.clone.sunk | while | flops 356000256 | bytes 38999928 | solution.py:86
  116.9 3.9 fusion.176
  120.8 5.7 convolution_add_fusion.4
  126.6 5.4 convolution_dynamic-update-slice_fusion.5
  132.0 3.5 fusion.177
  144.6 3.9 fusion.176
  148.6 5.9 convolution_add_fusion.4
  154.4 5.4 convolution_dynamic-update-slice_fusion.5
  159.8 3.5 fusion.177
  165.6 3.0 convolution_dynamic-update-slice_fusion.4
  172.5 3.9 fusion.176
  176.4 5.9 convolution_add_fusion.4
  182.3 5.4 convolution_dynamic-update-slice_fusion.5
  187.7 3.5 fusion.177
  200.3 3.9 fusion.176
  204.2 5.8 convolution_add_fusion.4
  210.1 5.4 convolution_dynamic-update-slice_fusion.5
  215.5 3.5 fusion.177
  228.1 3.9 fusion.176
  232.0 5.8 convolution_add_fusion.4
  237.9 5.4 convolution_dynamic-update-slice_fusion.5
  243.3 3.5 fusion.177
  255.9 3.9 fusion.176
  259.8 5.9 convolution_add_fusion.4
  265.7 5.4 convolution_dynamic-update-slice_fusion.5
  271.1 3.5 fusion.177
  283.8 3.9 fusion.176
  287.7 5.9 convolution_add_fusion.4
  293.5 5.4 convolution_dynamic-update-slice_fusion.5
  298.9 3.5 fusion.177
  311.6 3.9 fusion.176
  315.5 5.8 convolution_add_fusion.4
  321.4 5.4 convolution_dynamic-update-slice_fusion.5
  326.8 3.5 fusion.177
  346.0 53.0 %all-reduce.4.cloned.1.call-done = bf16[4,1024,128]{2,1,0:T(8,128)(2,1)} async-done(((bf16[4,1024,128]{2,1,0:T(8,128)(2,1)}), bf16[4,1024,128]{2,1,0:T(8,128)(2,1)}) %all-reduce.4.cloned.1.call-update) | async-done | bytes 1048592 | tf_op jit(solution)/shard_map/psum | solution.py:99
  399.0 3.3 convert_reduce_fusion.1
  402.4 3.3 fusion.69
  405.6 404.6 %reduce-scatter.2.cloned.1.call-done = f32[16,1024]{1,0:T(8,128)} async-done(((f32[1024,1024]{1,0:T(8,128)}), f32[16,1024]{1,0:T(8,128)}) %reduce-scatter.2.cloned.1.call-update) | async-done | bytes 65552 | tf_op jit(solution)/shard_map/reduce_scatter | solution.py:89
  810.3 5.7 fusion.81
  816.0 10.7 all-gather
  826.7 3.6 fusion.109
  831.9 401.8 %all-reduce = (f32[32,128]{1,0:T(8,128)}, f32[128,1]{0,1:T(1,128)}) all-reduce(f32[32,128]{1,0:T(8,128)S(1)} %convolution_bitcast_fusion.1, f32[128,1]{0,1:T(1,128)S(1)} %fusion.81), channel_id=1, replica_groups=mesh['rows'=64,'heads'=4] {'rows'}, use_global_device_ids=true, to_apply=%region_17.18 | all-reduce | flops 4224 | bytes 33792 | tf_op jit(solution)/shard_map/psum | solution.py:115
  1233.7 285.9 %all-reduce.6.cloned.1.call-done = f32[128,4,32]{0,2,1:T(8,128)} async-done(((f32[128,4,32]{0,2,1:T(8,128)}), f32[128,4,32]{0,2,1:T(8,128)}) %all-reduce.6.cloned.1.call-update) | async-done | bytes 65552 | tf_op jit(solution)/shard_map/psum | solution.py:115
  (201 shorter events, 93.7 us)
Async XLA Ops:
  7.2 22.5 %copy-start = (bf16[4,1024,128]{2,1,0:T(8,128)(2,1)S(1)}, bf16[4,1024,128]{2,1,0:T(8,128)(2,1)}, u32[]{:S(2)}) copy-start(bf16[4,1024,128]{2,1,0:T(8,128)(2,1)} %param.15) | copy-start | bytes 3145732
  7.2 102.5 %all-gather.3.cloned.1.call-start = ((), (), s32[]{:S(2)}) async-start(), calls=%async_computation.1 | async-start | bytes 2129920 | tf_op jit(solution)/shard_map/all_gather | solution.py:69
  13.7 3.4 copy-start.1
  18.4 4.4 copy-start.3
  21.9 3.2 copy-start.20
  22.5 376.5 %all-reduce.4.cloned.1.call-start = ((), (), s32[]{:S(2)}) async-start(), calls=%async_computation.2 | async-start | bytes 2097152 | tf_op jit(solution)/shard_map/psum | solution.py:99
  25.1 3.0 copy-start.12
  25.1 4.6 copy-start.26
  132.0 3.6 copy-start.10
  132.0 3.6 copy-start.14
  132.0 3.6 copy-start.23
  132.0 3.6 copy-start.27
  159.8 3.5 copy-start.10
  159.8 3.6 copy-start.14
  159.8 3.6 copy-start.23
  159.8 3.6 copy-start.27
  165.6 3.0 copy-start.11
  187.7 3.5 copy-start.10
  187.7 3.6 copy-start.14
  187.7 3.6 copy-start.23
  187.7 3.6 copy-start.27
  215.4 3.5 copy-start.10
  215.4 3.6 copy-start.14
  215.4 3.6 copy-start.23
  215.5 3.6 copy-start.27
  243.3 3.5 copy-start.10
  243.3 3.6 copy-start.14
  243.3 3.6 copy-start.23
  243.3 3.6 copy-start.27
  271.1 3.5 copy-start.10
  271.1 3.6 copy-start.14
  271.1 3.6 copy-start.23
  271.1 3.6 copy-start.27
  298.9 3.6 copy-start.10
  298.9 3.6 copy-start.14
  298.9 3.6 copy-start.23
  298.9 3.6 copy-start.27
  326.7 3.5 copy-start.10
  326.7 3.6 copy-start.14
  326.7 3.6 copy-start.23
  326.7 3.6 copy-start.27
  336.4 3.6 copy-start.21
  341.5 468.8 %reduce-scatter.2.cloned.1.call-start = ((), (), s32[]{:S(2)}) async-start(), calls=%async_computation.3 | async-start | bytes 4259840 | tf_op jit(solution)/shard_map/reduce_scatter | solution.py:89
  342.2 1177.3 %all-reduce.6.cloned.1.call-start = ((), (), s32[]{:S(2)}) async-start(), calls=%async_computation.4 | async-start | bytes 131072 | tf_op jit(solution)/shard_map/psum | solution.py:115
  399.0 3.3 copy-start.5
  810.3 5.7 copy-start.19
  810.3 16.4 %copy-start.2 = (bf16[16,1024,128]{1,2,0:T(8,128)(2,1)S(1)}, bf16[16,1024,128]{1,2,0:T(8,128)(2,1)}, u32[]{:S(2)}) copy-start(bf16[16,1024,128]{1,2,0:T(8,128)(2,1)} %copy.14) | copy-start | bytes 12582916
  810.3 16.4 %copy-start.25 = (bf16[128,4]{0,1:T(4,128)(2,1)S(1)}, bf16[128,4]{0,1:T(4,128)(2,1)}, u32[]{:S(2)}) copy-start(bf16[128,4]{0,1:T(4,128)(2,1)} %param.14) | copy-start | bytes 3076
  (19 other events, 40.5 us)
Sparse Core Ops, SparseCore 0:
  22.6 87.0 all-gather.2
  341.6 57.3 all-reduce.3
  401.7 408.5 reduce-scatter.1
  813.3 706.1 all-reduce.5
where the time goes:
time: 1530 us
  waiting for transfers between devices  823 us (54%)
  blocking collectives  412 us (27%)
  matrix products  223 us (15%)
  other arithmetic  32.1 us (2%)
  local copies, waits for them, and re-layouts  22.3 us (1%)
    reduce_scatter x1, waiting for transfers between devices, shards(): lax.psum_scatter(bias_part, 'rows', scatter_dimension=0, tiled=True)  405 us
    psum x1, blocking collectives, shards(): summed = lax.psum((dw_head, dwout_head, dwbias_head), 'rows')  402 us
    psum x1, waiting for transfers between devices, shards(): summed = lax.psum((dw_head, dwout_head, dwbias_head), 'rows')  286 us
    all_gather x1, waiting for transfers between devices, shards(): plane = lax.all_gather(bias_rows, 'rows', axis=0, tiled=True)  78.7 us
    psum x1, waiting for transfers between devices, shards(): lax.psum(dx_part.astype(jnp.bfloat16), 'heads').astype(jnp.float32)  53 us
    dot_general x8, matrix products, block_terms(): jnp.einsum('sjk,sjd->skd', logits_b, query_block, preferred_element_type=...  46.7 us
    dot_general x8, matrix products, block_terms(): jnp.einsum('sjk,skd->sjd', logits_b, key_vecs, preferred_element_type=jnp...  43.1 us
    sub x8, matrix products, block_terms(): expo = jnp.exp(logits - top)  31.5 us
  transfers between devices with their start and end apart: 4, of which 4 were waited for; matrix products, arithmetic and copies ran while one was open for 2% of the time, Pallas kernels for 0%

commit v1 on v0

v1 whole, which is shorter than its diff:
```python
import jax
import jax.numpy as jnp
from jax import lax
from jax.experimental import pallas as pl
from jax.experimental.pallas import tpu as pltpu
from jax.sharding import PartitionSpec as P

MESH = pl.DeviceIdType.MESH
F32 = jnp.float32
BF16 = jnp.bfloat16
N = 1024
C = 128
DH = 32
ROWS = 4
OWN = 16
BLK = 256
EPS = 1e-05
SCALE = 1.0 / DH**0.5


def nn(a, b):
    return lax.dot_general(a, b, (((1,), (0,)), ((), ())), preferred_element_type=F32)


def nt(a, b):
    return lax.dot_general(a, b, (((1,), (1,)), ((), ())), preferred_element_type=F32)


def norm_cols(t):
    cen = t - jnp.mean(t, axis=0, keepdims=True)
    r = lax.rsqrt(jnp.mean(cen * cen, axis=0, keepdims=True) + EPS)
    return cen * r, r


class Sems:
    def __init__(self):
        self.count = 0

    def take(self, n):
        first = self.count
        self.count += n
        return first


SEMS = Sems()
G1 = SEMS.take(1)
G2A = SEMS.take(4)
G2B = SEMS.take(4)
G3A = SEMS.take(4)
G3B = SEMS.take(4)
G4A = SEMS.take(4)
G4B = SEMS.take(4)
R1 = SEMS.take(4)
R2A = SEMS.take(4)
R2B = SEMS.take(4)
R3A = SEMS.take(4)
R3B = SEMS.take(4)
R4 = SEMS.take(1)
R5 = SEMS.take(4)
DXR = SEMS.take(16)
DXA = SEMS.take(16)
W1 = SEMS.take(1)
W2 = SEMS.take(4)
W3 = SEMS.take(4)
W4 = SEMS.take(1)
W5 = SEMS.take(1)
B1 = SEMS.take(1)
B2 = SEMS.take(4)
B3 = SEMS.take(4)
B4 = SEMS.take(1)


def kernel(
    slab, pair, mask, wt, wn, wout, wb, wq, wbar, dout,
    o_dslab, o_dpair, o_w, o_wb,
    plane, dbias, xpt, braw, yq, rp, own_bias, ys, rs, xst, zt, z, rhs, natt,
    dkv, gate_s, do_s, s1, r1, s2, r2a, r2b, s3, r3a, r3b, s4, r4, dbown, dbh, dball,
    dxs, dxr, dsl, wacc, w1r, wh, w2r, w3r, w4r, w5r, bsum, b1r, b2r, b3r, b4r,
    send, recv,
):
    r = lax.axis_index("rows")
    h = lax.axis_index("heads")
    c = lax.rem(r, 2)
    x = lax.rem(r // 2, 4)
    zh = lax.rem(r // 8, 2)
    y = r // 16

    def rid(y_, zh_, x_, c_):
        return ((y_ * 2 + zh_) * 4 + x_) * 2 + c_

    def off(a, d):
        return lax.rem(a + d, 4)

    core_peer = (rid(y, zh, x, 1 - c), h)
    zh_peer = (rid(y, 1 - zh, x, c), h)

    def x_peer(d):
        return (rid(y, zh, off(x, d), c), h)

    def y_peer(d):
        return (rid(off(y, d), zh, x, c), h)

    def h_peer(d):
        return (r, off(h, d))

    def copy(src, dst, sem, peer):
        return pltpu.make_async_remote_copy(
            src_ref=src, dst_ref=dst, send_sem=send.at[sem], recv_sem=recv.at[sem],
            device_id=peer, device_id_type=MESH,
        )

    barrier = pltpu.get_barrier_semaphore()
    peers = [core_peer, zh_peer]
    for d in (1, 2, 3):
        peers += [x_peer(d), y_peer(d), h_peer(d)]
    for peer in peers:
        pl.semaphore_signal(barrier, inc=1, device_id=peer, device_id_type=MESH)

    eye = (
        lax.broadcasted_iota(jnp.int32, (C, C), 0) == lax.broadcasted_iota(jnp.int32, (C, C), 1)
    ).astype(F32).astype(BF16)

    def pair_row(j, _):
        yt, rj = norm_cols(nt(eye, pair[j]))
        xb = yt.astype(BF16)
        xpt[j] = xb
        rp[pl.ds(j, 1), :] = rj
        ys[0] = yt
        yq[j] = ys[0, pl.ds(pl.multiple_of(h * DH, DH), DH), :]
        raw = nn(wb[...], xb)
        braw[j] = raw
        own_bias[pl.ds(j, 1), :] = raw[0:1, :]
        return 0

    lax.fori_loop(0, OWN, pair_row, 0)
    plane[y, zh, x, c] = own_bias[...].astype(BF16)
    pl.semaphore_wait(barrier, len(peers))

    g1 = copy(plane.at[y, zh, x, c], plane.at[y, zh, x, c], G1, zh_peer)
    g1.start()

    def slab_row(i, _):
        yt, ri = norm_cols(nt(eye, slab[i]))
        ys[i] = yt
        rs[pl.ds(i, 1), :] = ri
        xb = yt.astype(BF16)
        xst[i] = xb
        proj = nn(wt[...], xb)
        gate = 1.0 / (1.0 + jnp.exp(-proj[96:128]))
        do = nt(wout[...], dout[i])
        gate_s[i] = gate
        do_s[i] = do
        stack = jnp.concatenate([proj[0:96], do * gate], axis=0)
        zt[i] = stack.astype(BF16)
        z[i] = stack.T.astype(BF16)
        return 0

    g1.wait()
    g2 = []
    for d in (1, 2, 3):
        a = copy(plane.at[y, 0, x, c], plane.at[y, 0, x, c], G2A + d, x_peer(d))
        b = copy(plane.at[y, 1, x, c], plane.at[y, 1, x, c], G2B + d, y_peer(d))
        a.start()
        b.start()
        g2 += [a, b]
    lax.fori_loop(0, ROWS, slab_row, 0)
    wacc[...] = jnp.zeros(wacc.shape, F32)
    dball[...] = jnp.zeros(dball.shape, F32)
    rhs[...] = jnp.zeros(rhs.shape, BF16)
    for g in g2:
        g.wait()
    g3 = []
    for d in (1, 2, 3):
        a = copy(plane.at[y, 0, :, c], plane.at[y, 0, :, c], G3A + d, y_peer(d))
        b = copy(plane.at[:, 1, x, c], plane.at[:, 1, x, c], G3B + d, x_peer(d))
        a.start()
        b.start()
        g3 += [a, b]
    g4 = []

    def to_core(d):
        ya, xa = off(y + 4, -d), off(x + 4, -d)
        a = copy(plane.at[ya, 0, :, c], plane.at[ya, 0, :, c], G4A + d, core_peer)
        b = copy(plane.at[:, 1, xa, c], plane.at[:, 1, xa, c], G4B + d, core_peer)
        a.start()
        b.start()
        g4.extend([a, b])

    to_core(0)
    for d in (1, 2, 3):
        g3[2 * d - 2].wait_recv()
        g3[2 * d - 1].wait_recv()
        to_core(d)
    for g in g3:
        g.wait_send()
    for g in g4:
        g.wait()

    def r1_copy(yy):
        return copy(s1.at[yy], r1.at[yy], R1 + yy, core_peer)

    def block(i, keep, jb):
        rows = pl.ds(pl.multiple_of(jb * BLK, BLK), BLK)
        zj = z[i, rows, :]
        bias = plane[jb].reshape(BLK, N).astype(F32)
        logits = nn(zj, rhs[:, 0:N]) * SCALE + bias
        logits = jnp.where(keep, logits, -1e9)
        expo = jnp.exp(logits - jnp.max(logits, axis=1, keepdims=True))
        probs = expo * (1.0 / jnp.sum(expo, axis=1, keepdims=True))
        pb = probs.astype(BF16)
        dp = nn(zj, rhs[:, N : 2 * N])
        dl = probs * (dp - jnp.sum(probs * dp, axis=1, keepdims=True))
        dl = jnp.where(keep, dl, 0.0)
        dlb = dl.astype(BF16)
        dl6 = dl.reshape(2, 4, 2, OWN, N)

        @pl.when(i == 0)
        def _():
            dbias[jb] = dl6

        @pl.when(i > 0)
        def _():
            dbias[jb] += dl6

        zall = z[i]
        lane = lax.broadcasted_iota(jnp.int32, (BLK, C), 1)
        natt[rows, :] = jnp.where(lane < 64, nn(dlb, zall), nn(pb, zall))
        dkv[0:DH, :] += nn(zt[i, 0:DH, rows], dlb)
        dkv[DH:64, :] += nn(zt[i, 96:128, rows], pb)

        @pl.when(i == ROWS - 1)
        def _():
            s1[jb] = dbias[jb, :, :, 1 - c].astype(BF16)
            r1_copy(jb).start()

    def dx_copies(i):
        return [
            copy(dxs.at[i, off(h, d)], dxr.at[i, d], DXR + 4 * i + d, h_peer(d))
            for d in (1, 2, 3)
        ]

    def slab_copies(i):
        return [copy(dsl.at[i, h], dsl.at[i, h], DXA + 4 * i + d, h_peer(d)) for d in (1, 2, 3)]

    def finish_slab(i):
        for cp in dx_copies(i):
            cp.wait()
        g = dxs[i, h].astype(F32)
        for d in (1, 2, 3):
            g = g + dxr[i, d].astype(F32)
        cols = pl.ds(pl.multiple_of(h * BLK, BLK), BLK)
        yt = ys[i, :, cols]
        ri = rs[pl.ds(i, 1), cols]
        out = ri * (
            g - jnp.mean(g, axis=0, keepdims=True) - yt * jnp.mean(g * yt, axis=0, keepdims=True)
        )
        dsl[i, h] = out.T.astype(BF16)
        for cp in slab_copies(i):
            cp.start()

    def attend(i, _):
        keep = mask[pl.ds(i, 1), :] == 1
        rhs[0:DH, 0:N] = zt[i, 32:64, :]
        rhs[96:128, N : 2 * N] = zt[i, 64:96, :]
        dkv[...] = jnp.zeros(dkv.shape, F32)

        def step(jb, _):
            block(i, keep, jb)
            return 0

        lax.fori_loop(0, N // BLK, step, 0)
        nat = natt[...].T
        gate = gate_s[i]
        do = do_s[i]
        att = nat[64:96]
        gated = (gate * att).astype(BF16)
        dgate = do * att * gate * (1.0 - gate)
        grads = jnp.concatenate(
            [nat[32:64] * SCALE, dkv[0:DH, :] * SCALE, dkv[DH:64, :], dgate], axis=0
        ).astype(BF16)
        wacc[0:C, :] += nt(xst[i], grads)
        wacc[C : C + DH, :] += nn(gated, dout[i])
        dx = nn(wn[...], grads).astype(BF16)
        for q in range(4):
            dxs[i, q] = dx[:, q * BLK : (q + 1) * BLK]
        for cp in dx_copies(i):
            cp.start()

        @pl.when(i > 0)
        def _():
            finish_slab(i - 1)

        return 0

    lax.fori_loop(0, ROWS, attend, 0)

    half = pl.ds(pl.multiple_of(c * 80, 80), 80)
    other = pl.ds(pl.multiple_of((1 - c) * 80, 80), 80)
    w1 = copy(wacc.at[other], w1r, W1, core_peer)
    w1.start()
    r2 = []

    def r1_sum(yy):
        cp = r1_copy(yy)
        cp.wait()
        total = dbias[yy, :, :, c] + r1[yy].astype(F32)
        dbias[yy, :, :, c] = total
        s2[yy] = total.astype(BF16)

    for d in (1, 2, 3):
        r1_sum(off(y, d))
        a = copy(s2.at[off(y, d), 0], r2a.at[d], R2A + d, y_peer(d))
        a.start()
        r2.append(a)
    r1_sum(y)
    for d in (1, 2, 3):
        b = copy(s2.at[:, 1, off(x, d)], r2b.at[d], R2B + d, x_peer(d))
        b.start()
        r2.append(b)
    finish_slab(ROWS - 1)
    w1.wait()
    wh[0] = wacc[half, :] + w1r[...]
    w2 = [copy(wh.at[0], w2r.at[d], W2 + d, x_peer(d)) for d in (1, 2, 3)]
    for cp in w2:
        cp.start()
    for cp in r2:
        cp.wait()
    t0 = dbias[y, 0, :, c]
    t1 = dbias[:, 1, x, c]
    for d in (1, 2, 3):
        t0 = t0 + r2a[d].astype(F32)
        t1 = t1 + r2b[d].astype(F32)
    s3[0] = t0
    s3[1] = t1
    r3 = []
    for d in (1, 2, 3):
        a = copy(s3.at[0, off(x, d)], r3a.at[d], R3A + d, x_peer(d))
        b = copy(s3.at[1, off(y, d)], r3b.at[d], R3B + d, y_peer(d))
        a.start()
        b.start()
        r3 += [a, b]
    for cp in w2:
        cp.wait()
    wh[1] = wh[0] + w2r[1] + w2r[2] + w2r[3]
    w3 = [copy(wh.at[1], w3r.at[d], W3 + d, y_peer(d)) for d in (1, 2, 3)]
    for cp in w3:
        cp.start()
    for cp in r3:
        cp.wait()
    s4[0] = s3[0, x] + r3a[1] + r3a[2] + r3a[3]
    s4[1] = s3[1, y] + r3b[1] + r3b[2] + r3b[3]
    cp4 = copy(s4.at[1 - zh], r4, R4, zh_peer)
    cp4.start()
    for cp in w3:
        cp.wait()
    wh[2] = wh[1] + w3r[1] + w3r[2] + w3r[3]
    w4 = copy(wh.at[2], w4r, W4, zh_peer)
    w4.start()
    cp4.wait()
    db = s4[zh] + r4[...]
    dbb = db.astype(BF16)
    dbown[...] = dbb
    r5 = [copy(dbown, dbh.at[d], R5 + d, h_peer(d)) for d in (1, 2, 3)]
    for cp in r5:
        cp.start()

    own_bias[...] = db
    bsum[0] = jnp.zeros((OWN, C), F32)
    row_of = lax.broadcasted_iota(jnp.int32, (OWN, N), 0)

    def wb_row(j, _):
        picked = jnp.where(row_of == j, own_bias[...], 0.0)
        hi = picked.astype(BF16)
        lo = (picked - hi.astype(F32)).astype(BF16)
        bsum[0] += nt(hi, xpt[j]) + nt(lo, xpt[j])
        return 0

    lax.fori_loop(0, OWN, wb_row, 0)
    b1 = copy(bsum.at[0], b1r, B1, core_peer)
    b1.start()
    w4.wait()
    wh[3] = wh[2] + w4r[...]
    w5 = copy(wh.at[3], w5r, W5, core_peer)
    w5.start()
    b1.wait()
    bsum[1] = bsum[0] + b1r[...]
    b2 = [copy(bsum.at[1], b2r.at[d], B2 + d, x_peer(d)) for d in (1, 2, 3)]
    for cp in b2:
        cp.start()

    for cp in r5:
        cp.wait()
    dball[:, 0, :] = dbb.astype(F32)
    for d in (1, 2, 3):
        dball[:, d, :] = dbh[d].astype(F32)

    def dpair_row(j, _):
        dbj = dball[j]
        g = nn(wq[...], dbj.astype(BF16))
        first = jnp.sum(dbj * wbar[:, 0:1], axis=0, keepdims=True)
        second = jnp.sum(dbj * braw[j], axis=0, keepdims=True) * (1.0 / C)
        o_dpair[j] = (rp[pl.ds(j, 1), :] * (g - first - yq[j] * second)).astype(BF16)
        return 0

    lax.fori_loop(0, 8, dpair_row, 0)
    for cp in b2:
        cp.wait()
    bsum[2] = bsum[1] + b2r[1] + b2r[2] + b2r[3]
    b3 = [copy(bsum.at[2], b3r.at[d], B3 + d, y_peer(d)) for d in (1, 2, 3)]
    for cp in b3:
        cp.start()
    lax.fori_loop(8, OWN, dpair_row, 0)
    for cp in b3:
        cp.wait()
    bsum[3] = bsum[2] + b3r[1] + b3r[2] + b3r[3]
    b4 = copy(bsum.at[3], b4r, B4, zh_peer)
    b4.start()

    def slab_wait(i, _):
        for cp in slab_copies(i):
            cp.wait()
        return 0

    lax.fori_loop(0, ROWS, slab_wait, 0)
    for i in range(ROWS):
        for q in range(4):
            o_dslab[i, q * BLK : (q + 1) * BLK, :] = dsl[i, q]
    w5.wait()
    o_w[half, :] = wh[3]
    o_w[other, :] = w5r[...]
    b4.wait()
    o_wb[...] = bsum[3] + b4r[...]


def scratch():
    v = pltpu.VMEM
    return [
        v((4, 2, 4, 2, OWN, N), BF16),
        v((4, 2, 4, 2, OWN, N), F32),
        v((OWN, C, N), BF16),
        v((OWN, OWN, N), F32),
        v((OWN, DH, N), F32),
        v((OWN, N), F32),
        v((OWN, N), F32),
        v((ROWS, C, N), F32),
        v((8, N), F32),
        v((ROWS, C, N), BF16),
        v((ROWS, C, N), BF16),
        v((ROWS, N, C), BF16),
        v((C, 2 * N), BF16),
        v((N, C), F32),
        v((64, N), F32),
        v((ROWS, DH, N), F32),
        v((ROWS, DH, N), F32),
        v((4, 2, 4, OWN, N), BF16),
        v((4, 2, 4, OWN, N), BF16),
        v((4, 2, 4, OWN, N), BF16),
        v((4, 4, OWN, N), BF16),
        v((4, 4, OWN, N), BF16),
        v((2, 4, OWN, N), F32),
        v((4, OWN, N), F32),
        v((4, OWN, N), F32),
        v((2, OWN, N), F32),
        v((OWN, N), F32),
        v((OWN, N), BF16),
        v((4, OWN, N), BF16),
        v((OWN, OWN, N), F32),
        v((ROWS, 4, C, BLK), BF16),
        v((ROWS, 4, C, BLK), BF16),
        v((ROWS, 4, BLK, C), BF16),
        v((C + DH, C), F32),
        v((80, C), F32),
        v((4, 80, C), F32),
        v((4, 80, C), F32),
        v((4, 80, C), F32),
        v((80, C), F32),
        v((80, C), F32),
        v((4, OWN, C), F32),
        v((OWN, C), F32),
        v((4, OWN, C), F32),
        v((4, OWN, C), F32),
        v((OWN, C), F32),
        pltpu.SemaphoreType.DMA((SEMS.count,)),
        pltpu.SemaphoreType.DMA((SEMS.count,)),
    ]


def shards(slab, pair, pair_mask, w_qkvg, w_out, w_bias, d_out):
    head = lax.axis_index("heads")
    wn = w_qkvg.reshape(C, C)
    wt = wn.T
    order = lax.rem(head + 4 - jnp.arange(4), 4)
    wrel = jnp.take(w_bias, order, axis=1)
    wb = jnp.zeros((16, C), BF16).at[0:4].set(wrel.T)
    quarter = lax.dynamic_slice_in_dim(wrel, head * DH, DH, 0)
    wq = jnp.zeros((DH, 16), BF16).at[:, 0:4].set(quarter)
    mean = jnp.mean(wrel.astype(F32), axis=0)
    wbar = jnp.zeros((16, C), F32).at[0:4].set(jnp.broadcast_to(mean[:, None], (4, C)))
    vm = pl.BlockSpec(memory_space=pltpu.VMEM)
    d_slab, d_pair, w, wbg = pl.pallas_call(
        kernel,
        out_shape=(
            jax.ShapeDtypeStruct((ROWS, N, C), BF16),
            jax.ShapeDtypeStruct((OWN, DH, N), BF16),
            jax.ShapeDtypeStruct((C + DH, C), F32),
            jax.ShapeDtypeStruct((OWN, C), F32),
        ),
        in_specs=[vm] * 10,
        out_specs=(vm,) * 4,
        scratch_shapes=scratch(),
        compiler_params=pltpu.CompilerParams(
            collective_id=0, has_side_effects=True, vmem_limit_bytes=60 * 1024 * 1024
        ),
    )(slab, pair, pair_mask, wt, wn, w_out, wb, wq, wbar, d_out)
    return (
        d_slab,
        jnp.swapaxes(d_pair, 1, 2),
        w[0:C].reshape(C, 4, DH),
        w[C:],
        jnp.sum(wbg, axis=0)[:, None],
    )


def solution(mesh):
    placed = (
        P("rows", None, None),
        P("rows", None, None),
        P("rows", None),
        P(None, None, "heads"),
        P("heads", None),
        P(),
        P("rows", None, None),
    )
    return jax.shard_map(
        shards,
        mesh=mesh,
        in_specs=placed,
        out_specs=(
            P("rows", None, None),
            P("rows", None, "heads"),
            P(None, None, "heads"),
            P("heads", None),
            P(None, "heads"),
        ),
        check_vma=False,
    )
```

time: 1530 us -> 127 us (0.08)
  waiting for transfers between devices: 823 us -> 0 us
  blocking collectives: 412 us -> 0 us
  matrix products: 223 us -> 0 us
  Pallas kernels: 0 us -> 111 us
  other arithmetic: 32.1 us -> 2.61 us
    reduce_scatter x1 -> x0, waiting for transfers between devices: 405 us -> none  [shards(): lax.psum_scatter(bias_part, 'rows', scatter_dimension=0, tiled=True)]
    psum x1 -> x0, blocking collectives: 402 us -> none  [shards(): summed = lax.psum((dw_head, dwout_head, dwbias_head), 'rows')]
    psum x2 -> x0, waiting for transfers between devices: 339 us -> none  [the longest x1 286 us: shards(): summed = lax.psum((dw_head, dwout_head, dwbias_head), 'rows')]
    dot_general x48 -> x0, matrix products: 163 us -> none  [the longest x8 46.7 us: block_terms(): jnp.einsum('sjk,sjd->skd', logits_b, query_block, preferred_element_type=...]
    pallas_call x0 -> x1, Pallas kernels: none -> 111 us  [shards(): pl.pallas_call(kernel, out_shape=(jax.ShapeDtypeStruct((ROWS, N, C), BF16...]
    all_gather x1 -> x0, waiting for transfers between devices: 78.7 us -> none  [shards(): plane = lax.all_gather(bias_rows, 'rows', axis=0, tiled=True)]
    sub x16 -> x0, matrix products: 59.7 us -> none  [the longest x8 31.5 us: block_terms(): expo = jnp.exp(logits - top)]
    convert_element_type x11 -> x0, other arithmetic: 19.2 us -> none  [the longest x8 14.3 us: block_terms(): bias_block.astype(jnp.float32)[None]]
  transfers between devices with their start and end apart: 4 -> 0, of which waited for: 4 -> 0; matrix products, arithmetic and copies ran while one was open for 2% -> 0% of each run, Pallas kernels for 0% -> 0%
where the time goes in v1:
time: 127 us; the launch traced here: 126 us
  Pallas kernels  111 us (87%)
  local copies, waits for them, and re-layouts  11.6 us (9%)
  other arithmetic  2.61 us (2%)
    pallas_call x1, Pallas kernels, shards(): pl.pallas_call(kernel, out_shape=(jax.ShapeDtypeStruct((ROWS, N, C), BF16...  111 us
    unnamed x5, local copies, waits for them, and re-layouts  4.63 us

profile of v1, /device:TPU:1, one launch (start us, length us, event | category | flops | bytes accessed | tf_op | source)
XLA Modules:
  0.0 126.1 jit_solution(14231882162791741916)
XLA Ops:
  0.6 0.0 copy-start
  0.6 0.6 compare_reduce_fusion
  1.3 0.0 copy-done
  1.3 0.6 gather_fusion
  1.9 0.1 copy.17
  2.1 0.1 copy.21
  2.2 0.7 select_bitcast_fusion
  2.8 0.6 scatter.18.wq
  3.5 0.6 scatter.14.clone.wb
  4.0 0.7 scatter.20.wbar
  4.7 1.5 %copy.18.wn = bf16[128,128]{1,0:T(8,128)(2,1)} copy(bf16[128,128]{0,1:T(8,128)(2,1)} %bitcast.11) | data formatting | bytes 65536 | tf_op jit(solution)/shard_map/reshape | solution.py:490
  6.2 111.3 %shard_map.110 = (bf16[4,1024,128]{2,1,0:T(8,128)(2,1)}, bf16[16,32,1024]{2,1,0:T(8,128)(2,1)}, f32[160,128]{1,0:T(8,128)}, f32[16,128]{1,0:T(8,128)}) custom-call(bf16[4,1024,128]{2,1,0:T(8,128)(2,1)} %slab.1, bf16[16,1024,128]{2,1,0:T(8,128)(2,1)} %pair.1, s32[4,1024]{1,0:T(4,128)} %mask.1, bf16[128,128]{1,0:T(8,128)(2,1)} %bitcast.12, ...), custom_call_target="tpu_custom_call" | custom-call | tf_op jit(solution)/shard_map/pallas_call | solution.py:500
  117.5 1.2 reduce_sum.19
  118.7 1.3 %slice.55 = f32[32,128]{1,0:T(8,128)} slice(f32[160,128]{1,0:T(8,128)} %get-tuple-element.47), slice={[128:160], [0:128]} | slice | bytes 32768 | tf_op jit(solution)/shard_map/slice | solution.py:519
  120.0 0.8 slice.54
  120.9 0.7 copy.20
  121.6 2.3 %copy.24 = bf16[4,1024,128]{2,1,0:T(8,128)(2,1)} copy(bf16[4,1024,128]{2,1,0:T(8,128)(2,1)} %get-tuple-element.61) | data formatting | bytes 2097152
  123.8 2.3 %copy.25 = bf16[16,1024,32]{1,2,0:T(8,128)(2,1)} copy(bf16[16,1024,32]{1,2,0:T(8,128)(2,1)} %bitcast.10) | data formatting | bytes 2097152
  (6 shorter events, 0.1 us)
Async XLA Ops:
  0.6 0.7 copy-start

commit v2 on v0

v2 whole, which is shorter than its diff:
```python
import jax
import jax.numpy as jnp
from jax import lax
from jax.experimental import pallas as pl
from jax.experimental.pallas import tpu as pltpu
from jax.sharding import PartitionSpec as P

MESH = pl.DeviceIdType.MESH
F32 = jnp.float32
BF16 = jnp.bfloat16
N = 1024
C = 128
DH = 32
ROWS = 4
OWN = 16
BLK = 256
HALF = 512
EPS = 1e-05
SCALE = 1.0 / DH**0.5


def nn(a, b):
    return lax.dot_general(a, b, (((1,), (0,)), ((), ())), preferred_element_type=F32)


def nt(a, b):
    return lax.dot_general(a, b, (((1,), (1,)), ((), ())), preferred_element_type=F32)


def norm_cols(t):
    cen = t - jnp.mean(t, axis=0, keepdims=True)
    r = lax.rsqrt(jnp.mean(cen * cen, axis=0, keepdims=True) + EPS)
    return cen * r, r


class Sems:
    def __init__(self):
        self.count = 0

    def take(self, n):
        first = self.count
        self.count += n
        return first


SEMS = Sems()
G1 = SEMS.take(1)
GP = SEMS.take(32)
GC = SEMS.take(2)
R1 = SEMS.take(2)
R2 = SEMS.take(16)
R3 = SEMS.take(16)
R4 = SEMS.take(8)
DXR = SEMS.take(16)
DXA = SEMS.take(16)
W1 = SEMS.take(8)
W2 = SEMS.take(8)
W3 = SEMS.take(8)
B1 = SEMS.take(8)
B2 = SEMS.take(8)
LOW = slice(0, HALF)
HIGH = slice(HALF, N)


def kernel(
    slab_h, pair_h, mask, wt, wout, wbias, dout_h,
    o_dslab, o_dpair, o_dw, o_dwout, o_dwb,
    slab, pair, dout, wn, wbt, wb,
    plane, dbias, xpt, braw, yq, rp, own_bias, ys, rs, xst, zq, z, rhs, natt,
    dkv, gate_s, do_s, s1, r1, s2, r2a, r2b, s3, r3a, r3b, s4, r4, dball,
    dxs, dxr, dsl, wacc, w1r, wpart, w2r, wtot, fold, bsum, b1r, b2r,
    send, recv, load,
):
    r = lax.axis_index("rows")
    h = lax.axis_index("heads")
    c = lax.rem(r, 2)
    x = lax.rem(r // 2, 4)
    zh = lax.rem(r // 8, 2)
    y = r // 16
    oz = 1 - zh

    def off(a, d):
        return lax.rem(a + d, 4)

    def flip(a, e):
        return 1 - a if e else a

    def peer(dy=0, ez=0, dx=0, ec=0, dh=0):
        row = ((off(y, dy) * 2 + flip(zh, ez)) * 4 + off(x, dx)) * 2 + flip(c, ec)
        return (row, off(h, dh))

    def copy(src, dst, sem, to):
        return pltpu.make_async_remote_copy(
            src_ref=src, dst_ref=dst, send_sem=send.at[sem], recv_sem=recv.at[sem],
            device_id=to, device_id_type=MESH,
        )

    loads = [pltpu.make_async_copy(pair_h.at[4 * k : 4 * k + 4], pair.at[4 * k : 4 * k + 4], load.at[k]) for k in range(4)]
    loads.append(pltpu.make_async_copy(slab_h, slab, load.at[4]))
    loads.append(pltpu.make_async_copy(dout_h, dout, load.at[5]))
    for cp in loads:
        cp.start()

    near = [(dx, ec) for dx in range(4) for ec in range(2) if dx or ec]
    far = [(dy, ez) for dy in range(4) for ez in range(2) if dy or ez]
    peers = [peer(dx=a, ec=b) for a, b in near] + [peer(dy=a, ez=b) for a, b in far]
    for d in (1, 2, 3):
        peers += [peer(dh=d), peer(ez=1, dh=d)]
    barrier = pltpu.get_barrier_semaphore()
    for to in peers:
        pl.semaphore_signal(barrier, inc=1, device_id=to, device_id_type=MESH)

    eye = (
        lax.broadcasted_iota(jnp.int32, (C, C), 0) == lax.broadcasted_iota(jnp.int32, (C, C), 1)
    ).astype(F32).astype(BF16)

    wn[...] = nt(eye, wt[...]).astype(BF16)
    row16 = lax.broadcasted_iota(jnp.int32, (16, C), 0)
    heads = wbias[...].astype(F32)
    wrel = jnp.zeros((16, C), F32)
    for k in range(4):
        wrel = wrel + jnp.where(row16 == off(h + 4, -k), heads[k : k + 1, :], 0.0)
    wb[...] = wrel.astype(BF16)
    wbt[...] = nt(eye, wrel.astype(BF16))
    wbar = jnp.mean(wrel, axis=1, keepdims=True)

    def pair_row(j, _):
        yt, rj = norm_cols(nt(eye, pair[j]))
        xb = yt.astype(BF16)
        xpt[j] = xb
        rp[pl.ds(j, 1), :] = rj
        ys[lax.rem(j, 2)] = yt
        yq[j] = ys[lax.rem(j, 2), pl.ds(pl.multiple_of(h * DH, DH), DH), :]
        raw = nn(wb[...], xb)
        braw[j] = raw
        own_bias[pl.ds(j, 1), :] = raw[0:1, :]
        return 0

    for k in range(4):
        loads[k].wait()
        lax.fori_loop(4 * k, 4 * k + 4, pair_row, 0, unroll=True)
    plane[y, zh, x, c] = own_bias[...].astype(BF16)
    pl.semaphore_wait(barrier, len(peers))

    def gather_first(s):
        zs = flip(zh, s)
        out = []
        for d in (1, 2, 3):
            low = plane.at[y, zs, x, c, :, LOW]
            high = plane.at[y, zs, x, c, :, HIGH]
            out.append(copy(low, low, GP + 16 * s + d, peer(dx=d)))
            out.append(copy(high, high, GP + 16 * s + 4 + d, peer(dy=d)))
        return out

    def gather_second(s):
        zs = flip(zh, s)
        out = []
        for d in (1, 2, 3):
            low = plane.at[y, zs, :, c, :, LOW]
            high = plane.at[:, zs, x, c, :, HIGH]
            out.append(copy(low, low, GP + 16 * s + 8 + d, peer(dy=d)))
            out.append(copy(high, high, GP + 16 * s + 12 + d, peer(dx=d)))
        return out

    def gather_core(s):
        zs = flip(zh, s)
        return copy(plane.at[:, zs, :, c], plane.at[:, zs, :, c], GC + s, peer(ec=1))

    def begin(copies):
        for cp in copies:
            cp.start()

    def end(copies):
        for cp in copies:
            cp.wait()

    g1 = copy(plane.at[y, zh, x, c], plane.at[y, zh, x, c], G1, peer(ez=1))
    g1.start()
    ga1 = gather_first(0)
    begin(ga1)

    def slab_row(i, _):
        yt, ri = norm_cols(nt(eye, slab[i]))
        ys[i] = yt
        rs[pl.ds(i, 1), :] = ri
        xb = yt.astype(BF16)
        xst[i] = xb
        proj = nn(wt[...], xb)
        gate = 1.0 / (1.0 + jnp.exp(-proj[96:128]))
        do = nt(wout[...], dout[i])
        gate_s[i] = gate
        do_s[i] = do
        datt = do * gate
        stack = jnp.concatenate([proj[0:96], datt], axis=0)
        z[i] = stack.T.astype(BF16).reshape(4, 2, 128, C)
        both = jnp.concatenate([proj[0:DH], datt], axis=0).astype(BF16)
        for k in range(8):
            zq[i, k] = both[:, k * 128 : (k + 1) * 128]
        rhs[i, 0:DH, 0:N] = proj[32:64].astype(BF16)
        rhs[i, 96:128, N : 2 * N] = proj[64:96].astype(BF16)
        return 0

    rhs[...] = jnp.zeros(rhs.shape, BF16)
    loads[4].wait()
    loads[5].wait()
    lax.fori_loop(0, 2, slab_row, 0)
    end(ga1)
    ga2 = gather_second(0)
    begin(ga2)
    g1.wait()
    gb1 = gather_first(1)
    begin(gb1)
    lax.fori_loop(2, ROWS, slab_row, 0)
    wacc[...] = jnp.zeros(wacc.shape, F32)
    dkv[...] = jnp.zeros(dkv.shape, F32)
    dbias[...] = jnp.zeros(dbias.shape, F32)
    end(gb1)
    gb2 = gather_second(1)
    begin(gb2)
    end(ga2)
    gac = gather_core(0)
    gac.start()
    gac.wait()

    def block(i, yy, zs):
        keep = mask[pl.ds(i, 1), :] == 1
        two = pl.ds(2 * yy, 2)
        zj = z[i, two, zs].reshape(BLK, C)
        bias = plane[two, zs].reshape(BLK, N).astype(F32)
        logits = nn(zj, rhs[i, :, 0:N]) * SCALE + bias
        logits = jnp.where(keep, logits, -1e9)
        expo = jnp.exp(logits - jnp.max(logits, axis=1, keepdims=True))
        probs = expo * (1.0 / jnp.sum(expo, axis=1, keepdims=True))
        pb = probs.astype(BF16)
        dp = nn(zj, rhs[i, :, N : 2 * N])
        dl = probs * (dp - jnp.sum(probs * dp, axis=1, keepdims=True))
        dl = jnp.where(keep, dl, 0.0)
        dlb = dl.astype(BF16)
        dbias[two, zs] += dl.reshape(2, 4, 2, OWN, N)
        zall = z[i].reshape(N, C)
        lane = lax.broadcasted_iota(jnp.int32, (BLK, C), 1)
        nat = jnp.where(lane < 64, nn(dlb, zall), nn(pb, zall))
        natt[i, two, zs] = nat.reshape(2, 128, C)
        left = jnp.concatenate([zq[i, 4 * yy + zs], zq[i, 4 * yy + 2 + zs]], axis=1)
        dkv[i, 0:DH, :] += nn(left[0:DH], dlb)
        dkv[i, DH:64, :] += nn(left[DH:64], pb)

    def own_half(t, _):
        block(t // 2, lax.rem(t, 2), zh)
        return 0

    def other_half(t, _):
        block(t // 2, lax.rem(t, 2), oz)
        return 0

    def dx_copies(i):
        return [
            copy(dxs.at[i, off(h, d)], dxr.at[i, d], DXR + 4 * i + d, peer(dh=d))
            for d in (1, 2, 3)
        ]

    def slab_copies(i):
        return [copy(dsl.at[i, h], dsl.at[i, h], DXA + 4 * i + d, peer(dh=d)) for d in (1, 2, 3)]

    def finish_slab(i):
        end(dx_copies(i))
        g = dxs[i, h].astype(F32)
        for d in (1, 2, 3):
            g = g + dxr[i, d].astype(F32)
        cols = pl.ds(pl.multiple_of(h * BLK, BLK), BLK)
        yt = ys[i, :, cols]
        ri = rs[pl.ds(i, 1), cols]
        out = ri * (
            g - jnp.mean(g, axis=0, keepdims=True) - yt * jnp.mean(g * yt, axis=0, keepdims=True)
        )
        dsl[i, h] = out.T.astype(BF16)
        begin(slab_copies(i))

    def finish_row(i):
        nat = natt[i].reshape(N, C).T
        gate = gate_s[i]
        do = do_s[i]
        att = nat[64:96]
        gated = (gate * att).astype(BF16)
        dgate = do * att * gate * (1.0 - gate)
        grads = jnp.concatenate(
            [nat[32:64] * SCALE, dkv[i, 0:DH, :] * SCALE, dkv[i, DH:64, :], dgate], axis=0
        ).astype(BF16)
        dx = nn(wn[...], grads).astype(BF16)
        for q in range(4):
            dxs[i, q] = dx[:, q * BLK : (q + 1) * BLK]
        begin(dx_copies(i))
        wacc[0:C, :] += nt(grads, xst[i])
        wacc[C : C + DH, :] += nn(gated, dout[i])

    def sum_core(s):
        zs = flip(zh, s)
        s1[s] = dbias[:, zs, :, 1 - c].astype(BF16)
        return copy(s1.at[s], r1.at[s], R1 + s, peer(ec=1))

    def sum_first(s):
        zs = flip(zh, s)
        for yy in range(4):
            total = dbias[yy, zs, :, c] + r1[s, yy].astype(F32)
            dbias[yy, zs, :, c] = total
            s2[s, yy] = total.astype(BF16)
        out = []
        for d in (1, 2, 3):
            low = s2.at[s, off(y, d), :, :, LOW]
            high = s2.at[s, :, off(x, d), :, HIGH]
            out.append(copy(low, r2a.at[s, d], R2 + 8 * s + d, peer(dy=d)))
            out.append(copy(high, r2b.at[s, d], R2 + 8 * s + 4 + d, peer(dx=d)))
        return out

    def sum_second(s):
        zs = flip(zh, s)
        low = dbias[y, zs, :, c, :, LOW]
        high = dbias[:, zs, x, c, :, HIGH]
        for d in (1, 2, 3):
            low = low + r2a[s, d].astype(F32)
            high = high + r2b[s, d].astype(F32)
        s3[s, 0] = low.astype(BF16)
        s3[s, 1] = high.astype(BF16)
        dbias[y, zs, :, c, :, LOW] = low
        dbias[:, zs, x, c, :, HIGH] = high
        out = []
        for d in (1, 2, 3):
            out.append(copy(s3.at[s, 0, off(x, d)], r3a.at[s, d], R3 + 8 * s + d, peer(dx=d)))
            out.append(copy(s3.at[s, 1, off(y, d)], r3b.at[s, d], R3 + 8 * s + 4 + d, peer(dy=d)))
        return out

    def sum_last(s):
        zs = flip(zh, s)
        low = dbias[y, zs, x, c, :, LOW]
        high = dbias[y, zs, x, c, :, HIGH]
        for d in (1, 2, 3):
            low = low + r3a[s, d].astype(F32)
            high = high + r3b[s, d].astype(F32)
        both = jnp.concatenate([low, high], axis=1)
        s4[s] = both.astype(BF16)
        out = []
        for d in range(4):
            if s or d:
                out.append(copy(s4.at[s], r4.at[s, d], R4 + 4 * s + d, peer(ez=s, dh=d)))
        return both, out

    lax.fori_loop(0, 4, own_half, 0)
    end(gb2)
    gbc = gather_core(1)
    gbc.start()
    lax.fori_loop(4, 8, own_half, 0)
    ra1 = sum_core(0)
    ra1.start()
    gbc.wait()
    lax.fori_loop(0, 2, other_half, 0)
    finish_row(0)
    ra1.wait()
    ra2 = sum_first(0)
    begin(ra2)
    lax.fori_loop(2, 4, other_half, 0)
    finish_row(1)
    lax.fori_loop(4, 6, other_half, 0)
    finish_row(2)
    end(ra2)
    ra3 = sum_second(0)
    begin(ra3)
    lax.fori_loop(6, 8, other_half, 0)
    rb1 = sum_core(1)
    rb1.start()
    finish_row(3)
    chunk = 24

    def wslice(k):
        return pl.ds(pl.multiple_of(k * chunk, 8), chunk)

    def wid(dx, ec):
        return off(x, dx) * 2 + flip(c, ec)

    w1 = [
        copy(wacc.at[wslice(wid(a, b))], w1r.at[2 * a + b], W1 + 2 * a + b, peer(dx=a, ec=b))
        for a, b in near
    ]
    rb1.wait()
    rb2 = sum_first(1)
    begin(rb2)
    begin(w1)
    finish_slab(0)
    end(ra3)
    own, ra4 = sum_last(0)
    own_bias[...] = own
    begin(ra4)
    end(w1)
    part = wacc[wslice(wid(0, 0)), :]
    for a, b in near:
        part = part + w1r[2 * a + b]
    wpart[...] = part
    w2 = [copy(wpart, w2r.at[2 * a + b], W2 + 2 * a + b, peer(dy=a, ez=b)) for a, b in far]
    begin(w2)
    end(rb2)
    rb3 = sum_second(1)
    begin(rb3)
    finish_slab(1)
    end(rb3)
    _, rb4 = sum_last(1)
    begin(rb4)
    end(w2)
    part = wpart[...]
    for a, b in far:
        part = part + w2r[2 * a + b]
    wtot[wslice(wid(0, 0)), :] = part
    w3 = [
        copy(
            wtot.at[wslice(wid(0, 0))], wtot.at[wslice(wid(0, 0))], W3 + 2 * a + b,
            peer(dx=a, ec=b),
        )
        for a, b in near
    ]
    begin(w3)
    finish_slab(2)
    end(ra4)
    end(rb4)

    db = own_bias[...] + r4[1, 0].astype(F32)
    own_bias[...] = db
    dball[:, 0, :] = db
    for d in (1, 2, 3):
        dball[:, d, :] = r4[0, d].astype(F32) + r4[1, d].astype(F32)
    dball[:, 4:16, :] = jnp.zeros((OWN, 12, N), F32)

    def wb_part(k, _):
        sub = pl.ds(pl.multiple_of(k * 32, 32), 32)
        acc = xpt[0, sub, :].astype(F32) * own_bias[0:1, :]
        for j in range(1, OWN):
            acc = acc + xpt[j, sub, :].astype(F32) * own_bias[j : j + 1, :]
        total = acc[:, 0:128]
        for q in range(1, 8):
            total = total + acc[:, q * 128 : (q + 1) * 128]
        fold[sub, :] = total
        return 0

    lax.fori_loop(0, 4, wb_part, 0)
    total = fold[...]
    hi = total.astype(BF16)
    mid = (total - hi.astype(F32)).astype(BF16)
    lo = (total - hi.astype(F32) - mid.astype(F32)).astype(BF16)
    ones = jnp.ones((16, C), F32).astype(BF16)
    bsum[0] = (nt(ones, hi) + nt(ones, mid) + nt(ones, lo))[0:8]
    b1 = [copy(bsum.at[0], b1r.at[2 * a + b], B1 + 2 * a + b, peer(dx=a, ec=b)) for a, b in near]
    begin(b1)

    def dpair_row(j, _):
        dbj = dball[j]
        wq = wbt[pl.ds(pl.multiple_of(h * DH, DH), DH), :].astype(BF16)
        g = nn(wq, dbj.astype(BF16))
        first = jnp.sum(dbj * wbar, axis=0, keepdims=True)
        second = jnp.sum(dbj * braw[j], axis=0, keepdims=True) * (1.0 / C)
        o_dpair[j] = (rp[pl.ds(j, 1), :] * (g - first - yq[j] * second)).astype(BF16)
        return 0

    finish_slab(3)
    lax.fori_loop(0, 8, dpair_row, 0, unroll=4)
    end(b1)
    part = bsum[0]
    for a, b in near:
        part = part + b1r[2 * a + b]
    bsum[1] = part
    b2 = [copy(bsum.at[1], b2r.at[2 * a + b], B2 + 2 * a + b, peer(dy=a, ez=b)) for a, b in far]
    begin(b2)
    lax.fori_loop(8, OWN, dpair_row, 0, unroll=4)
    end(w3)
    o_dw[...] = wtot[0:C, :]
    o_dwout[...] = wtot[C : C + DH, :]
    for i in range(ROWS):
        end(slab_copies(i))
        for q in range(4):
            o_dslab[i, q * BLK : (q + 1) * BLK, :] = dsl[i, q]
    end(b2)
    part = bsum[1]
    for a, b in far:
        part = part + b2r[2 * a + b]
    o_dwb[...] = part[0:1, :]


def scratch():
    v = pltpu.VMEM
    return [
        v((ROWS, N, C), BF16),
        v((OWN, N, C), BF16),
        v((ROWS, N, C), BF16),
        v((C, C), BF16),
        v((C, 16), F32),
        v((16, C), BF16),
        v((4, 2, 4, 2, OWN, N), BF16),
        v((4, 2, 4, 2, OWN, N), F32),
        v((OWN, C, N), BF16),
        v((OWN, OWN, N), F32),
        v((OWN, DH, N), F32),
        v((OWN, N), F32),
        v((OWN, N), F32),
        v((ROWS, C, N), F32),
        v((8, N), F32),
        v((ROWS, C, N), BF16),
        v((ROWS, 8, 64, 128), BF16),
        v((ROWS, 4, 2, 128, C), BF16),
        v((ROWS, C, 2 * N), BF16),
        v((ROWS, 4, 2, 128, C), F32),
        v((ROWS, 64, N), F32),
        v((ROWS, DH, N), F32),
        v((ROWS, DH, N), F32),
        v((2, 4, 4, OWN, N), BF16),
        v((2, 4, 4, OWN, N), BF16),
        v((2, 4, 4, OWN, N), BF16),
        v((2, 4, 4, OWN, HALF), BF16),
        v((2, 4, 4, OWN, HALF), BF16),
        v((2, 2, 4, OWN, HALF), BF16),
        v((2, 4, OWN, HALF), BF16),
        v((2, 4, OWN, HALF), BF16),
        v((2, OWN, N), BF16),
        v((2, 4, OWN, N), BF16),
        v((OWN, OWN, N), F32),
        v((ROWS, 4, C, BLK), BF16),
        v((ROWS, 4, C, BLK), BF16),
        v((ROWS, 4, BLK, C), BF16),
        v((192, C), F32),
        v((8, 24, C), F32),
        v((24, C), F32),
        v((8, 24, C), F32),
        v((192, C), F32),
        v((C, C), F32),
        v((2, 8, C), F32),
        v((8, 8, C), F32),
        v((8, 8, C), F32),
        pltpu.SemaphoreType.DMA((SEMS.count,)),
        pltpu.SemaphoreType.DMA((SEMS.count,)),
        pltpu.SemaphoreType.DMA((6,)),
    ]


def hand_on(*refs):
    n = len(refs) // 2
    copies = [pltpu.make_async_copy(refs[k], refs[n + k], refs[-1].at[k]) for k in range(n)]
    for cp in copies:
        cp.start()
    for cp in copies:
        cp.wait()


def shards(slab, pair, pair_mask, w_qkvg, w_out, w_bias, d_out):
    wt = jnp.transpose(w_qkvg, (1, 2, 0)).reshape(C, C)
    vm = pl.BlockSpec(memory_space=pltpu.VMEM)
    anywhere = pl.BlockSpec(memory_space=pl.ANY)
    shapes = (
        jax.ShapeDtypeStruct((ROWS, N, C), BF16),
        jax.ShapeDtypeStruct((OWN, DH, N), BF16),
        jax.ShapeDtypeStruct((C, C), F32),
        jax.ShapeDtypeStruct((DH, C), F32),
        jax.ShapeDtypeStruct((1, C), F32),
    )
    outs = pl.pallas_call(
        kernel,
        out_shape=shapes,
        in_specs=[anywhere, anywhere, vm, vm, vm, vm, anywhere],
        out_specs=(vm,) * 5,
        scratch_shapes=scratch(),
        compiler_params=pltpu.CompilerParams(
            collective_id=0, has_side_effects=True, vmem_limit_bytes=60 * 1024 * 1024
        ),
    )(slab, pair, pair_mask, wt, w_out, w_bias.T, d_out)
    d_slab, d_pair, dw, dwout, dwb = pl.pallas_call(
        hand_on,
        out_shape=shapes,
        in_specs=[pl.BlockSpec(memory_space=pltpu.HBM)] * 5,
        out_specs=(anywhere,) * 5,
        scratch_shapes=[pltpu.SemaphoreType.DMA((5,))],
    )(*outs)
    return (
        d_slab,
        jnp.swapaxes(d_pair, 1, 2),
        jnp.transpose(dw.reshape(4, DH, C), (2, 0, 1)),
        dwout,
        dwb.T,
    )


def solution(mesh):
    placed = (
        P("rows", None, None),
        P("rows", None, None),
        P("rows", None),
        P(None, None, "heads"),
        P("heads", None),
        P(),
        P("rows", None, None),
    )
    return jax.shard_map(
        shards,
        mesh=mesh,
        in_specs=placed,
        out_specs=(
            P("rows", None, None),
            P("rows", None, "heads"),
            P(None, None, "heads"),
            P("heads", None),
            P(None, "heads"),
        ),
        check_vma=False,
    )
```

time: 1530 us -> 171 us (0.11)
  waiting for transfers between devices: 823 us -> 0 us
  blocking collectives: 412 us -> 0 us
  matrix products: 223 us -> 0 us
  Pallas kernels: 0 us -> 170 us
  other arithmetic: 32.1 us -> 0 us
  local copies, waits for them, and re-layouts: 22.3 us -> 0 us
    reduce_scatter x1 -> x0, waiting for transfers between devices: 405 us -> none  [shards(): lax.psum_scatter(bias_part, 'rows', scatter_dimension=0, tiled=True)]
    psum x1 -> x0, blocking collectives: 402 us -> none  [shards(): summed = lax.psum((dw_head, dwout_head, dwbias_head), 'rows')]
    psum x2 -> x0, waiting for transfers between devices: 339 us -> none  [the longest x1 286 us: shards(): summed = lax.psum((dw_head, dwout_head, dwbias_head), 'rows')]
    pallas_call x0 -> x2, Pallas kernels: none -> 170 us  [the longest x1 103 us: shards(): pl.pallas_call(kernel, out_shape=shapes, in_specs=[anywhere, anywhere, vm...]
    dot_general x48 -> x0, matrix products: 163 us -> none  [the longest x8 46.7 us: block_terms(): jnp.einsum('sjk,sjd->skd', logits_b, query_block, preferred_element_type=...]
    all_gather x1 -> x0, waiting for transfers between devices: 78.7 us -> none  [shards(): plane = lax.all_gather(bias_rows, 'rows', axis=0, tiled=True)]
    sub x16 -> x0, matrix products: 59.7 us -> none  [the longest x8 31.5 us: block_terms(): expo = jnp.exp(logits - top)]
    convert_element_type x11 -> x0, other arithmetic: 19.2 us -> none  [the longest x8 14.3 us: block_terms(): bias_block.astype(jnp.float32)[None]]
  transfers between devices with their start and end apart: 4 -> 0, of which waited for: 4 -> 0; matrix products, arithmetic and copies ran while one was open for 2% -> 0% of each run, Pallas kernels for 0% -> 0%
where the time goes in v2:
time: 171 us
  Pallas kernels  170 us (99%)
    pallas_call x1, Pallas kernels, shards(): pl.pallas_call(kernel, out_shape=shapes, in_specs=[anywhere, anywhere, vm...  103 us
    pallas_call x1, Pallas kernels, shards(): pl.pallas_call(hand_on, out_shape=shapes, in_specs=[pl.BlockSpec(memory_s...  67.2 us

profile of v2, /device:TPU:1, one launch (start us, length us, event | category | flops | bytes accessed | tf_op | source)
XLA Modules:
  0.0 171.0 jit_solution(3585447724996338521)
XLA Ops:
  0.6 103.1 %shard_map.110 = (bf16[4,1024,128]{2,1,0:T(8,128)(2,1)}, bf16[16,32,1024]{2,1,0:T(8,128)(2,1)}, f32[128,128]{1,0:T(8,128)}, f32[32,128]{1,0:T(8,128)}, f32[1,128]{1,0:T(1,128)}) custom-call(bf16[4,1024,128]{2,1,0:T(8,128)(2,1)} %slab_h.1, bf16[16,1024,128]{2,1,0:T(8,128)(2,1)} %pair_h.1, s32[4,1024]{1,0:T(4,128)} %mask.1, bf16[128,128]{1,0:T(8,128)(2,1)} %bitcast.9, ...), custom_call_target="tpu_custom_call" | custom-call | tf_op jit(solution)/shard_map/pallas_call | solution.py:559
  103.7 67.2 %shard_map.111 = (bf16[4,1024,128]{2,1,0:T(8,128)(2,1)}, bf16[16,32,1024]{2,1,0:T(8,128)(2,1)}, f32[128,128]{1,0:T(8,128)}, f32[32,128]{1,0:T(8,128)}, f32[1,128]{1,0:T(1,128)}) custom-call(bf16[4,1024,128]{2,1,0:T(8,128)(2,1)} %get-tuple-element.15.refs_0_, bf16[16,32,1024]{2,1,0:T(8,128)(2,1)} %get-tuple-element.16.refs_1_, ...), custom_call_target="tpu_custom_call" | custom-call | tf_op jit(solution)/shard_map/pallas_call | solution.py:569

commit v3 on v2

--- a/solution.py
+++ b/solution.py
@@ -51,7 +51,8 @@
 R2 = SEMS.take(16)
 R3 = SEMS.take(16)
 R4 = SEMS.take(8)
-DXR = SEMS.take(16)
+DX1 = SEMS.take(4)
+DX2 = SEMS.take(4)
 DXA = SEMS.take(16)
 W1 = SEMS.take(8)
 W2 = SEMS.take(8)
@@ -68,7 +69,7 @@
     slab, pair, dout, wn, wbt, wb,
     plane, dbias, xpt, braw, yq, rp, own_bias, ys, rs, xst, zq, z, rhs, natt,
     dkv, gate_s, do_s, s1, r1, s2, r2a, r2b, s3, r3a, r3b, s4, r4, dball,
-    dxs, dxr, dsl, wacc, w1r, wpart, w2r, wtot, fold, bsum, b1r, b2r,
+    dxs, dxr1, dxc, dxr2, dsl, wacc, w1r, wpart, w2r, wtot, fold, bsum, b1r, b2r,
     send, recv, load,
 ):
     r = lax.axis_index("rows")
@@ -78,6 +79,8 @@
     zh = lax.rem(r // 8, 2)
     y = r // 16
     oz = 1 - zh
+    odd = lax.rem(h, 2)
+    up = h // 2
 
     def off(a, d):
         return lax.rem(a + d, 4)
@@ -227,12 +230,12 @@
         two = pl.ds(2 * yy, 2)
         zj = z[i, two, zs].reshape(BLK, C)
         bias = plane[two, zs].reshape(BLK, N).astype(F32)
-        logits = nn(zj, rhs[i, :, 0:N]) * SCALE + bias
+        logits = nn(zj[:, 0:DH], rhs[i, 0:DH, 0:N]) * SCALE + bias
         logits = jnp.where(keep, logits, -1e9)
         expo = jnp.exp(logits - jnp.max(logits, axis=1, keepdims=True))
         probs = expo * (1.0 / jnp.sum(expo, axis=1, keepdims=True))
         pb = probs.astype(BF16)
-        dp = nn(zj, rhs[i, :, N : 2 * N])
+        dp = nn(zj[:, 96:128], rhs[i, 96:128, N : 2 * N])
         dl = probs * (dp - jnp.sum(probs * dp, axis=1, keepdims=True))
         dl = jnp.where(keep, dl, 0.0)
         dlb = dl.astype(BF16)
@@ -253,20 +256,24 @@
         block(t // 2, lax.rem(t, 2), oz)
         return 0
 
-    def dx_copies(i):
-        return [
-            copy(dxs.at[i, off(h, d)], dxr.at[i, d], DXR + 4 * i + d, peer(dh=d))
-            for d in (1, 2, 3)
-        ]
+    def dx_pair(i):
+        to = (r, h + 1 - 2 * odd)
+        return copy(dxs.at[i, 1 - odd], dxr1.at[i], DX1 + i, to)
+
+    def dx_cross(i):
+        return copy(dxc.at[i], dxr2.at[i], DX2 + i, (r, h + 2 - 4 * up))
+
+    def middle_slab(i):
+        dx_pair(i).wait()
+        dxc[i] = (dxs[i, odd, 1 - up].astype(F32) + dxr1[i, 1 - up].astype(F32)).astype(BF16)
+        dx_cross(i).start()
 
     def slab_copies(i):
         return [copy(dsl.at[i, h], dsl.at[i, h], DXA + 4 * i + d, peer(dh=d)) for d in (1, 2, 3)]
 
     def finish_slab(i):
-        end(dx_copies(i))
-        g = dxs[i, h].astype(F32)
-        for d in (1, 2, 3):
-            g = g + dxr[i, d].astype(F32)
+        dx_cross(i).wait()
+        g = dxs[i, odd, up].astype(F32) + dxr1[i, up].astype(F32) + dxr2[i].astype(F32)
         cols = pl.ds(pl.multiple_of(h * BLK, BLK), BLK)
         yt = ys[i, :, cols]
         ri = rs[pl.ds(i, 1), cols]
@@ -288,8 +295,8 @@
         ).astype(BF16)
         dx = nn(wn[...], grads).astype(BF16)
         for q in range(4):
-            dxs[i, q] = dx[:, q * BLK : (q + 1) * BLK]
-        begin(dx_copies(i))
+            dxs[i, q % 2, q // 2] = dx[:, q * BLK : (q + 1) * BLK]
+        dx_pair(i).start()
         wacc[0:C, :] += nt(grads, xst[i])
         wacc[C : C + DH, :] += nn(gated, dout[i])
 
@@ -344,27 +351,30 @@
                 out.append(copy(s4.at[s], r4.at[s, d], R4 + 4 * s + d, peer(ez=s, dh=d)))
         return both, out
 
-    lax.fori_loop(0, 4, own_half, 0)
+    lax.fori_loop(0, 4, own_half, 0, unroll=2)
     end(gb2)
     gbc = gather_core(1)
     gbc.start()
-    lax.fori_loop(4, 8, own_half, 0)
+    gbc.wait()
+    lax.fori_loop(0, 2, other_half, 0, unroll=2)
+    finish_row(0)
+    lax.fori_loop(4, 8, own_half, 0, unroll=2)
     ra1 = sum_core(0)
     ra1.start()
-    gbc.wait()
-    lax.fori_loop(0, 2, other_half, 0)
-    finish_row(0)
+    middle_slab(0)
+    lax.fori_loop(2, 4, other_half, 0, unroll=2)
+    finish_row(1)
     ra1.wait()
     ra2 = sum_first(0)
     begin(ra2)
-    lax.fori_loop(2, 4, other_half, 0)
-    finish_row(1)
-    lax.fori_loop(4, 6, other_half, 0)
+    finish_slab(0)
+    lax.fori_loop(4, 6, other_half, 0, unroll=2)
     finish_row(2)
     end(ra2)
     ra3 = sum_second(0)
     begin(ra3)
-    lax.fori_loop(6, 8, other_half, 0)
+    middle_slab(1)
+    lax.fori_loop(6, 8, other_half, 0, unroll=2)
     rb1 = sum_core(1)
     rb1.start()
     finish_row(3)
@@ -380,15 +390,16 @@
         copy(wacc.at[wslice(wid(a, b))], w1r.at[2 * a + b], W1 + 2 * a + b, peer(dx=a, ec=b))
         for a, b in near
     ]
+    end(ra3)
+    own, ra4 = sum_last(0)
+    own_bias[...] = own
+    begin(ra4)
     rb1.wait()
     rb2 = sum_first(1)
     begin(rb2)
     begin(w1)
-    finish_slab(0)
-    end(ra3)
-    own, ra4 = sum_last(0)
-    own_bias[...] = own
-    begin(ra4)
+    middle_slab(2)
+    finish_slab(1)
     end(w1)
     part = wacc[wslice(wid(0, 0)), :]
     for a, b in near:
@@ -396,13 +407,15 @@
     wpart[...] = part
     w2 = [copy(wpart, w2r.at[2 * a + b], W2 + 2 * a + b, peer(dy=a, ez=b)) for a, b in far]
     begin(w2)
+    middle_slab(3)
     end(rb2)
     rb3 = sum_second(1)
     begin(rb3)
-    finish_slab(1)
+    finish_slab(2)
     end(rb3)
     _, rb4 = sum_last(1)
     begin(rb4)
+    finish_slab(3)
     end(w2)
     part = wpart[...]
     for a, b in far:
@@ -416,7 +429,6 @@
         for a, b in near
     ]
     begin(w3)
-    finish_slab(2)
     end(ra4)
     end(rb4)
 
@@ -457,7 +469,6 @@
         o_dpair[j] = (rp[pl.ds(j, 1), :] * (g - first - yq[j] * second)).astype(BF16)
         return 0
 
-    finish_slab(3)
     lax.fori_loop(0, 8, dpair_row, 0, unroll=4)
     end(b1)
     part = bsum[0]
@@ -518,8 +529,10 @@
         v((2, OWN, N), BF16),
         v((2, 4, OWN, N), BF16),
         v((OWN, OWN, N), F32),
-        v((ROWS, 4, C, BLK), BF16),
-        v((ROWS, 4, C, BLK), BF16),
+        v((ROWS, 2, 2, C, BLK), BF16),
+        v((ROWS, 2, C, BLK), BF16),
+        v((ROWS, C, BLK), BF16),
+        v((ROWS, C, BLK), BF16),
         v((ROWS, 4, BLK, C), BF16),
         v((192, C), F32),
         v((8, 24, C), F32),
@@ -538,11 +551,8 @@
 
 def hand_on(*refs):
     n = len(refs) // 2
-    copies = [pltpu.make_async_copy(refs[k], refs[n + k], refs[-1].at[k]) for k in range(n)]
-    for cp in copies:
-        cp.start()
-    for cp in copies:
-        cp.wait()
+    for k in range(n):
+        refs[n + k][...] = refs[k][...]
 
 
 def shards(slab, pair, pair_mask, w_qkvg, w_out, w_bias, d_out):
@@ -566,12 +576,19 @@
             collective_id=0, has_side_effects=True, vmem_limit_bytes=60 * 1024 * 1024
         ),
     )(slab, pair, pair_mask, wt, w_out, w_bias.T, d_out)
+    blocks = [
+        pl.BlockSpec((1, N, C), lambda k: (k, 0, 0)),
+        pl.BlockSpec((4, DH, N), lambda k: (k, 0, 0)),
+        pl.BlockSpec((DH, C), lambda k: (k, 0)),
+        pl.BlockSpec((8, C), lambda k: (k, 0)),
+        pl.BlockSpec((1, C), lambda k: (0, 0)),
+    ]
     d_slab, d_pair, dw, dwout, dwb = pl.pallas_call(
         hand_on,
+        grid=(4,),
         out_shape=shapes,
-        in_specs=[pl.BlockSpec(memory_space=pltpu.HBM)] * 5,
-        out_specs=(anywhere,) * 5,
-        scratch_shapes=[pltpu.SemaphoreType.DMA((5,))],
+        in_specs=blocks,
+        out_specs=blocks,
     )(*outs)
     return (
         d_slab,

time: 171 us -> 106 us (0.62)
  Pallas kernels: 170 us -> 105 us
    pallas_call x1, Pallas kernels: 67.2 us -> 3.79 us  [shards(): pl.pallas_call(hand_on, grid=(4,), out_shape=shapes, in_specs=blocks, out...]
    pallas_call x1, Pallas kernels: 103 us -> 101 us  [shards(): pl.pallas_call(kernel, out_shape=shapes, in_specs=[anywhere, anywhere, vm...]
where the time goes in v3:
time: 106 us; the launch traced here: 105 us
  Pallas kernels  105 us (99%)
    pallas_call x1, Pallas kernels, shards(): pl.pallas_call(kernel, out_shape=shapes, in_specs=[anywhere, anywhere, vm...  101 us
    pallas_call x1, Pallas kernels, shards(): pl.pallas_call(hand_on, grid=(4,), out_shape=shapes, in_specs=blocks, out...  3.79 us

profile of v3, /device:TPU:1, one launch (start us, length us, event | category | flops | bytes accessed | tf_op | source)
XLA Modules:
  0.0 105.4 jit_solution(7037716883241919745)
XLA Ops:
  0.6 100.8 %shard_map.110 = (bf16[4,1024,128]{2,1,0:T(8,128)(2,1)}, bf16[16,32,1024]{2,1,0:T(8,128)(2,1)}, f32[128,128]{1,0:T(8,128)}, f32[32,128]{1,0:T(8,128)}, f32[1,128]{1,0:T(1,128)}) custom-call(bf16[4,1024,128]{2,1,0:T(8,128)(2,1)} %slab_h.1, bf16[16,1024,128]{2,1,0:T(8,128)(2,1)} %pair_h.1, s32[4,1024]{1,0:T(4,128)} %mask.1, bf16[128,128]{1,0:T(8,128)(2,1)} %bitcast.9, ...), custom_call_target="tpu_custom_call" | custom-call | tf_op jit(solution)/shard_map/pallas_call | solution.py:569
  101.4 3.8 %shard_map.111 = (bf16[4,1024,128]{2,1,0:T(8,128)(2,1)}, bf16[16,32,1024]{2,1,0:T(8,128)(2,1)}, f32[128,128]{1,0:T(8,128)}, f32[32,128]{1,0:T(8,128)}, f32[1,128]{1,0:T(1,128)}) custom-call(bf16[4,1024,128]{2,1,0:T(8,128)(2,1)} %get-tuple-element.15.refs_0_, bf16[16,32,1024]{2,1,0:T(8,128)(2,1)} %get-tuple-element.16.refs_1_, ...), custom_call_target="tpu_custom_call" | custom-call | tf_op jit(solution)/shard_map/pallas_call | solution.py:586

commit v4 on v3

--- a/solution.py
+++ b/solution.py
@@ -69,7 +69,7 @@
     slab, pair, dout, wn, wbt, wb,
     plane, dbias, xpt, braw, yq, rp, own_bias, ys, rs, xst, zq, z, rhs, natt,
     dkv, gate_s, do_s, s1, r1, s2, r2a, r2b, s3, r3a, r3b, s4, r4, dball,
-    dxs, dxr1, dxc, dxr2, dsl, wacc, w1r, wpart, w2r, wtot, fold, bsum, b1r, b2r,
+    dxs, dxr1, dxc, dxr2, dsl, dpair, wacc, w1r, wpart, w2r, wtot, fold, bsum, b1r, b2r,
     send, recv, load,
 ):
     r = lax.axis_index("rows")
@@ -351,30 +351,27 @@
                 out.append(copy(s4.at[s], r4.at[s, d], R4 + 4 * s + d, peer(ez=s, dh=d)))
         return both, out
 
+    def own_row(i):
+        lax.fori_loop(2 * i, 2 * i + 2, own_half, 0, unroll=2)
+
+    def other_row(i):
+        lax.fori_loop(2 * i, 2 * i + 2, other_half, 0, unroll=2)
+
     lax.fori_loop(0, 4, own_half, 0, unroll=2)
     end(gb2)
     gbc = gather_core(1)
     gbc.start()
+    own_row(2)
     gbc.wait()
-    lax.fori_loop(0, 2, other_half, 0, unroll=2)
-    finish_row(0)
-    lax.fori_loop(4, 8, own_half, 0, unroll=2)
+    for i in range(3):
+        other_row(i)
+        finish_row(i)
+    middle_slab(0)
+    own_row(3)
+    middle_slab(1)
     ra1 = sum_core(0)
     ra1.start()
-    middle_slab(0)
-    lax.fori_loop(2, 4, other_half, 0, unroll=2)
-    finish_row(1)
-    ra1.wait()
-    ra2 = sum_first(0)
-    begin(ra2)
-    finish_slab(0)
-    lax.fori_loop(4, 6, other_half, 0, unroll=2)
-    finish_row(2)
-    end(ra2)
-    ra3 = sum_second(0)
-    begin(ra3)
-    middle_slab(1)
-    lax.fori_loop(6, 8, other_half, 0, unroll=2)
+    other_row(3)
     rb1 = sum_core(1)
     rb1.start()
     finish_row(3)
@@ -390,16 +387,21 @@
         copy(wacc.at[wslice(wid(a, b))], w1r.at[2 * a + b], W1 + 2 * a + b, peer(dx=a, ec=b))
         for a, b in near
     ]
-    end(ra3)
-    own, ra4 = sum_last(0)
-    own_bias[...] = own
-    begin(ra4)
     rb1.wait()
     rb2 = sum_first(1)
     begin(rb2)
     begin(w1)
     middle_slab(2)
+    finish_slab(0)
     finish_slab(1)
+    ra1.wait()
+    ra2 = sum_first(0)
+    middle_slab(3)
+    end(rb2)
+    rb3 = sum_second(1)
+    begin(rb3)
+    begin(ra2)
+    finish_slab(2)
     end(w1)
     part = wacc[wslice(wid(0, 0)), :]
     for a, b in near:
@@ -407,15 +409,13 @@
     wpart[...] = part
     w2 = [copy(wpart, w2r.at[2 * a + b], W2 + 2 * a + b, peer(dy=a, ez=b)) for a, b in far]
     begin(w2)
-    middle_slab(3)
-    end(rb2)
-    rb3 = sum_second(1)
-    begin(rb3)
-    finish_slab(2)
     end(rb3)
     _, rb4 = sum_last(1)
     begin(rb4)
     finish_slab(3)
+    end(ra2)
+    ra3 = sum_second(0)
+    begin(ra3)
     end(w2)
     part = wpart[...]
     for a, b in far:
@@ -429,15 +429,14 @@
         for a, b in near
     ]
     begin(w3)
-    end(ra4)
-    end(rb4)
-
-    db = own_bias[...] + r4[1, 0].astype(F32)
+    end(ra3)
+    own, ra4 = sum_last(0)
+    begin(ra4)
+    rb4[0].wait()
+
+    db = own + r4[1, 0].astype(F32)
     own_bias[...] = db
     dball[:, 0, :] = db
-    for d in (1, 2, 3):
-        dball[:, d, :] = r4[0, d].astype(F32) + r4[1, d].astype(F32)
-    dball[:, 4:16, :] = jnp.zeros((OWN, 12, N), F32)
 
     def wb_part(k, _):
         sub = pl.ds(pl.multiple_of(k * 32, 32), 32)
@@ -466,10 +465,17 @@
         g = nn(wq, dbj.astype(BF16))
         first = jnp.sum(dbj * wbar, axis=0, keepdims=True)
         second = jnp.sum(dbj * braw[j], axis=0, keepdims=True) * (1.0 / C)
-        o_dpair[j] = (rp[pl.ds(j, 1), :] * (g - first - yq[j] * second)).astype(BF16)
+        dpair[j] = (rp[pl.ds(j, 1), :] * (g - first - yq[j] * second)).astype(BF16)
         return 0
 
+    end(ra4)
+    end(rb4[1:])
+    for d in (1, 2, 3):
+        dball[:, d, :] = r4[0, d].astype(F32) + r4[1, d].astype(F32)
+    dball[:, 4:16, :] = jnp.zeros((OWN, 12, N), F32)
     lax.fori_loop(0, 8, dpair_row, 0, unroll=4)
+    out_low = pltpu.make_async_copy(dpair.at[0:8], o_dpair.at[0:8], load.at[4])
+    out_low.start()
     end(b1)
     part = bsum[0]
     for a, b in near:
@@ -478,18 +484,22 @@
     b2 = [copy(bsum.at[1], b2r.at[2 * a + b], B2 + 2 * a + b, peer(dy=a, ez=b)) for a, b in far]
     begin(b2)
     lax.fori_loop(8, OWN, dpair_row, 0, unroll=4)
+    out_high = pltpu.make_async_copy(dpair.at[8:16], o_dpair.at[8:16], load.at[5])
+    out_high.start()
     end(w3)
     o_dw[...] = wtot[0:C, :]
     o_dwout[...] = wtot[C : C + DH, :]
+    slab_out = [pltpu.make_async_copy(dsl.at[i], o_dslab.at[i], load.at[i]) for i in range(ROWS)]
     for i in range(ROWS):
         end(slab_copies(i))
-        for q in range(4):
-            o_dslab[i, q * BLK : (q + 1) * BLK, :] = dsl[i, q]
+        slab_out[i].start()
     end(b2)
     part = bsum[1]
     for a, b in far:
         part = part + b2r[2 * a + b]
     o_dwb[...] = part[0:1, :]
+    for cp in slab_out + [out_low, out_high]:
+        cp.wait()
 
 
 def scratch():
@@ -534,6 +544,7 @@
         v((ROWS, C, BLK), BF16),
         v((ROWS, C, BLK), BF16),
         v((ROWS, 4, BLK, C), BF16),
+        v((OWN, DH, N), BF16),
         v((192, C), F32),
         v((8, 24, C), F32),
         v((24, C), F32),
@@ -550,9 +561,24 @@
 
 
 def hand_on(*refs):
-    n = len(refs) // 2
-    for k in range(n):
-        refs[n + k][...] = refs[k][...]
+    outs, held, sem = refs[5:10], refs[10:15], refs[15]
+    first, second = [], []
+    for k in range(5):
+        pieces = 4 if k < 2 else 1
+        for q in range(pieces):
+            size = held[k].shape[0] // pieces
+            part = pl.ds(q * size, size)
+            one = sem.at[0, 4 * k + q]
+            two = sem.at[1, 4 * k + q]
+            first.append(pltpu.make_async_copy(refs[k].at[part], held[k].at[part], one))
+            second.append(pltpu.make_async_copy(held[k].at[part], outs[k].at[part], two))
+    for cp in first:
+        cp.start()
+    for cp, then in zip(first, second):
+        cp.wait()
+        then.start()
+    for cp in second:
+        cp.wait()
 
 
 def shards(slab, pair, pair_mask, w_qkvg, w_out, w_bias, d_out):
@@ -560,7 +586,7 @@
     vm = pl.BlockSpec(memory_space=pltpu.VMEM)
     anywhere = pl.BlockSpec(memory_space=pl.ANY)
     shapes = (
-        jax.ShapeDtypeStruct((ROWS, N, C), BF16),
+        jax.ShapeDtypeStruct((ROWS, 4, BLK, C), BF16),
         jax.ShapeDtypeStruct((OWN, DH, N), BF16),
         jax.ShapeDtypeStruct((C, C), F32),
         jax.ShapeDtypeStruct((DH, C), F32),
@@ -570,28 +596,23 @@
         kernel,
         out_shape=shapes,
         in_specs=[anywhere, anywhere, vm, vm, vm, vm, anywhere],
-        out_specs=(vm,) * 5,
+        out_specs=(anywhere, anywhere, vm, vm, vm),
         scratch_shapes=scratch(),
         compiler_params=pltpu.CompilerParams(
             collective_id=0, has_side_effects=True, vmem_limit_bytes=60 * 1024 * 1024
         ),
     )(slab, pair, pair_mask, wt, w_out, w_bias.T, d_out)
-    blocks = [
-        pl.BlockSpec((1, N, C), lambda k: (k, 0, 0)),
-        pl.BlockSpec((4, DH, N), lambda k: (k, 0, 0)),
-        pl.BlockSpec((DH, C), lambda k: (k, 0)),
-        pl.BlockSpec((8, C), lambda k: (k, 0)),
-        pl.BlockSpec((1, C), lambda k: (0, 0)),
-    ]
+    in_hbm = pl.BlockSpec(memory_space=pltpu.HBM)
     d_slab, d_pair, dw, dwout, dwb = pl.pallas_call(
         hand_on,
-        grid=(4,),
         out_shape=shapes,
-        in_specs=blocks,
-        out_specs=blocks,
+        in_specs=[in_hbm] * 5,
+        out_specs=(in_hbm,) * 5,
+        scratch_shapes=[pltpu.VMEM(one.shape, one.dtype) for one in shapes]
+        + [pltpu.SemaphoreType.DMA((2, 20))],
     )(*outs)
     return (
-        d_slab,
+        d_slab.reshape(ROWS, N, C),
         jnp.swapaxes(d_pair, 1, 2),
         jnp.transpose(dw.reshape(4, DH, C), (2, 0, 1)),
         dwout,

time: 106 us -> 99.9 us (0.942)
  Pallas kernels: 105 us -> 98.8 us
    pallas_call x1, Pallas kernels: 101 us -> 96.2 us  [shards(): pl.pallas_call(kernel, out_shape=shapes, in_specs=[anywhere, anywhere, vm...]
    pallas_call x1, Pallas kernels: 3.79 us -> 2.63 us  [shards(): pl.pallas_call(hand_on, out_shape=shapes, in_specs=[in_hbm] * 5, out_spec...]
where the time goes in v4:
time: 99.9 us; the launch traced here: 99.6 us
  Pallas kernels  98.8 us (99%)
    pallas_call x1, Pallas kernels, shards(): pl.pallas_call(kernel, out_shape=shapes, in_specs=[anywhere, anywhere, vm...  96.2 us
    pallas_call x1, Pallas kernels, shards(): pl.pallas_call(hand_on, out_shape=shapes, in_specs=[in_hbm] * 5, out_spec...  2.63 us

profile of v4, /device:TPU:1, one launch (start us, length us, event | category | flops | bytes accessed | tf_op | source)
XLA Modules:
  0.0 99.6 jit_solution(7051031074982936130)
XLA Ops:
  0.6 96.2 %shard_map.110 = (bf16[4,4,256,128]{3,2,1,0:T(8,128)(2,1)}, bf16[16,32,1024]{2,1,0:T(8,128)(2,1)}, f32[128,128]{1,0:T(8,128)}, f32[32,128]{1,0:T(8,128)}, f32[1,128]{1,0:T(1,128)}) custom-call(bf16[4,1024,128]{2,1,0:T(8,128)(2,1)} %slab_h.1, bf16[16,1024,128]{2,1,0:T(8,128)(2,1)} %pair_h.1, s32[4,1024]{1,0:T(4,128)} %mask.1, bf16[128,128]{1,0:T(8,128)(2,1)} %bitcast.10, ...), custom_call_target="tpu_custom_call" | custom-call | tf_op jit(solution)/shard_map/pallas_call | solution.py:595
  96.8 2.6 %shard_map.111 = (bf16[4,4,256,128]{3,2,1,0:T(8,128)(2,1)}, bf16[16,32,1024]{2,1,0:T(8,128)(2,1)}, f32[128,128]{1,0:T(8,128)}, f32[32,128]{1,0:T(8,128)}, f32[1,128]{1,0:T(1,128)}) custom-call(bf16[4,4,256,128]{3,2,1,0:T(8,128)(2,1)} %get-tuple-element.15.refs_0_, bf16[16,32,1024]{2,1,0:T(8,128)(2,1)} %get-tuple-element.16.refs_1_, ...), custom_call_target="tpu_custom_call" | custom-call | tf_op jit(solution)/shard_map/pallas_call | solution.py:606

commit v5 on v4

--- a/solution.py
+++ b/solution.py
@@ -51,9 +51,10 @@
 R2 = SEMS.take(16)
 R3 = SEMS.take(16)
 R4 = SEMS.take(8)
-DX1 = SEMS.take(4)
-DX2 = SEMS.take(4)
-DXA = SEMS.take(16)
+S1 = SEMS.take(8)
+S2 = SEMS.take(4)
+T1 = SEMS.take(8)
+T2 = SEMS.take(4)
 W1 = SEMS.take(8)
 W2 = SEMS.take(8)
 W3 = SEMS.take(8)
@@ -69,7 +70,7 @@
     slab, pair, dout, wn, wbt, wb,
     plane, dbias, xpt, braw, yq, rp, own_bias, ys, rs, xst, zq, z, rhs, natt,
     dkv, gate_s, do_s, s1, r1, s2, r2a, r2b, s3, r3a, r3b, s4, r4, dball,
-    dxs, dxr1, dxc, dxr2, dsl, dpair, wacc, w1r, wpart, w2r, wtot, fold, bsum, b1r, b2r,
+    dxs, e1, dxc, e2, dsl, dpair, wacc, w1r, wpart, w2r, wtot, fold, bsum, b1r, b2r,
     send, recv, load,
 ):
     r = lax.axis_index("rows")
@@ -79,8 +80,13 @@
     zh = lax.rem(r // 8, 2)
     y = r // 16
     oz = 1 - zh
-    odd = lax.rem(h, 2)
-    up = h // 2
+    inner = (h == 1) | (h == 2)
+    at_end = jnp.logical_not(inner)
+    side = h // 2
+    mine = jnp.where(inner, h - 1, 0)
+    to_inner = (r, jnp.where(inner, 3 - h, 1 + side))
+    to_end = (r, jnp.where(h == 1, 0, 3))
+    to_other = (r, 3 - h)
 
     def off(a, d):
         return lax.rem(a + d, 4)
@@ -256,32 +262,70 @@
         block(t // 2, lax.rem(t, 2), oz)
         return 0
 
-    def dx_pair(i):
-        to = (r, h + 1 - 2 * odd)
-        return copy(dxs.at[i, 1 - odd], dxr1.at[i], DX1 + i, to)
-
-    def dx_cross(i):
-        return copy(dxc.at[i], dxr2.at[i], DX2 + i, (r, h + 2 - 4 * up))
+    def up_copies(i):
+        far_half = 1 - side
+        return [
+            copy(dxs.at[i, far_half], e1.at[i, far_half], S1 + 2 * i, to_inner),
+            copy(dxs.at[i, side], e1.at[i, side], S1 + 2 * i + 1, to_inner),
+        ]
+
+    def cross_copy(i):
+        return copy(dxc.at[i], e2.at[i], S2 + i, to_other)
+
+    def done_copies(i):
+        return [
+            copy(dsl.at[i, mine], dsl.at[i, mine], T1 + 2 * i, to_other),
+            copy(dsl.at[i, mine], dsl.at[i, mine], T1 + 2 * i + 1, to_end),
+        ]
+
+    def pass_copy(i):
+        return copy(dsl.at[i, 1 - mine], dsl.at[i, 1 - mine], T2 + i, to_end)
+
+    def send_row(i):
+        @pl.when(at_end)
+        def _():
+            begin(up_copies(i))
 
     def middle_slab(i):
-        dx_pair(i).wait()
-        dxc[i] = (dxs[i, odd, 1 - up].astype(F32) + dxr1[i, 1 - up].astype(F32)).astype(BF16)
-        dx_cross(i).start()
-
-    def slab_copies(i):
-        return [copy(dsl.at[i, h], dsl.at[i, h], DXA + 4 * i + d, peer(dh=d)) for d in (1, 2, 3)]
+        @pl.when(inner)
+        def _():
+            up_copies(i)[0].wait_recv()
+            g = dxs[i, 1 - mine].astype(F32) + e1[i, 1 - mine].astype(F32)
+            dxc[i] = g.astype(BF16)
+            cross_copy(i).start()
 
     def finish_slab(i):
-        dx_cross(i).wait()
-        g = dxs[i, odd, up].astype(F32) + dxr1[i, up].astype(F32) + dxr2[i].astype(F32)
-        cols = pl.ds(pl.multiple_of(h * BLK, BLK), BLK)
-        yt = ys[i, :, cols]
-        ri = rs[pl.ds(i, 1), cols]
-        out = ri * (
-            g - jnp.mean(g, axis=0, keepdims=True) - yt * jnp.mean(g * yt, axis=0, keepdims=True)
-        )
-        dsl[i, h] = out.T.astype(BF16)
-        begin(slab_copies(i))
+        @pl.when(inner)
+        def _():
+            up_copies(i)[1].wait_recv()
+            cross_copy(i).wait()
+            g = dxs[i, mine].astype(F32) + e1[i, mine].astype(F32) + e2[i].astype(F32)
+            cols = pl.ds(pl.multiple_of(mine * HALF, HALF), HALF)
+            yt = ys[i, :, cols]
+            ri = rs[pl.ds(i, 1), cols]
+            first = jnp.mean(g, axis=0, keepdims=True)
+            out = ri * (g - first - yt * jnp.mean(g * yt, axis=0, keepdims=True))
+            dsl[i, mine] = out.T.astype(BF16)
+            begin(done_copies(i))
+
+    def pass_slab(i):
+        @pl.when(inner)
+        def _():
+            done_copies(i)[0].wait_recv()
+            pass_copy(i).start()
+
+    def end_slab(i):
+        @pl.when(inner)
+        def _():
+            for cp in done_copies(i) + [pass_copy(i)]:
+                cp.wait_send()
+
+        @pl.when(at_end)
+        def _():
+            for cp in up_copies(i):
+                cp.wait_send()
+            done_copies(i)[1].wait_recv()
+            pass_copy(i).wait_recv()
 
     def finish_row(i):
         nat = natt[i].reshape(N, C).T
@@ -294,9 +338,9 @@
             [nat[32:64] * SCALE, dkv[i, 0:DH, :] * SCALE, dkv[i, DH:64, :], dgate], axis=0
         ).astype(BF16)
         dx = nn(wn[...], grads).astype(BF16)
-        for q in range(4):
-            dxs[i, q % 2, q // 2] = dx[:, q * BLK : (q + 1) * BLK]
-        dx_pair(i).start()
+        dxs[i, 0] = dx[:, LOW]
+        dxs[i, 1] = dx[:, HIGH]
+        send_row(i)
         wacc[0:C, :] += nt(grads, xst[i])
         wacc[C : C + DH, :] += nn(gated, dout[i])
 
@@ -361,16 +405,19 @@
     end(gb2)
     gbc = gather_core(1)
     gbc.start()
-    own_row(2)
     gbc.wait()
-    for i in range(3):
+    for i in range(2):
         other_row(i)
         finish_row(i)
+    own_row(2)
     middle_slab(0)
+    other_row(2)
+    finish_row(2)
+    middle_slab(1)
     own_row(3)
-    middle_slab(1)
     ra1 = sum_core(0)
     ra1.start()
+    finish_slab(0)
     other_row(3)
     rb1 = sum_core(1)
     rb1.start()
@@ -391,16 +438,16 @@
     rb2 = sum_first(1)
     begin(rb2)
     begin(w1)
+    finish_slab(1)
+    pass_slab(0)
     middle_slab(2)
-    finish_slab(0)
-    finish_slab(1)
     ra1.wait()
     ra2 = sum_first(0)
-    middle_slab(3)
     end(rb2)
     rb3 = sum_second(1)
     begin(rb3)
     begin(ra2)
+    pass_slab(1)
     finish_slab(2)
     end(w1)
     part = wacc[wslice(wid(0, 0)), :]
@@ -409,13 +456,44 @@
     wpart[...] = part
     w2 = [copy(wpart, w2r.at[2 * a + b], W2 + 2 * a + b, peer(dy=a, ez=b)) for a, b in far]
     begin(w2)
+    middle_slab(3)
     end(rb3)
     _, rb4 = sum_last(1)
     begin(rb4)
-    finish_slab(3)
     end(ra2)
     ra3 = sum_second(0)
     begin(ra3)
+    pass_slab(2)
+    finish_slab(3)
+    end(ra3)
+    own, ra4 = sum_last(0)
+    begin(ra4)
+    rb4[0].wait()
+
+    db = own + r4[1, 0].astype(F32)
+    own_bias[...] = db
+    dball[:, 0, :] = db
+
+    def wb_part(k, _):
+        sub = pl.ds(pl.multiple_of(k * 32, 32), 32)
+        acc = xpt[0, sub, :].astype(F32) * own_bias[0:1, :]
+        for j in range(1, OWN):
+            acc = acc + xpt[j, sub, :].astype(F32) * own_bias[j : j + 1, :]
+        total = acc[:, 0:128]
+        for q in range(1, 8):
+            total = total + acc[:, q * 128 : (q + 1) * 128]
+        fold[sub, :] = total
+        return 0
+
+    lax.fori_loop(0, 4, wb_part, 0)
+    total = fold[...]
+    hi = total.astype(BF16)
+    mid = (total - hi.astype(F32)).astype(BF16)
+    lo = (total - hi.astype(F32) - mid.astype(F32)).astype(BF16)
+    ones = jnp.ones((16, C), F32).astype(BF16)
+    bsum[0] = (nt(ones, hi) + nt(ones, mid) + nt(ones, lo))[0:8]
+    b1 = [copy(bsum.at[0], b1r.at[2 * a + b], B1 + 2 * a + b, peer(dx=a, ec=b)) for a, b in near]
+    begin(b1)
     end(w2)
     part = wpart[...]
     for a, b in far:
@@ -429,35 +507,6 @@
         for a, b in near
     ]
     begin(w3)
-    end(ra3)
-    own, ra4 = sum_last(0)
-    begin(ra4)
-    rb4[0].wait()
-
-    db = own + r4[1, 0].astype(F32)
-    own_bias[...] = db
-    dball[:, 0, :] = db
-
-    def wb_part(k, _):
-        sub = pl.ds(pl.multiple_of(k * 32, 32), 32)
-        acc = xpt[0, sub, :].astype(F32) * own_bias[0:1, :]
-        for j in range(1, OWN):
-            acc = acc + xpt[j, sub, :].astype(F32) * own_bias[j : j + 1, :]
-        total = acc[:, 0:128]
-        for q in range(1, 8):
-            total = total + acc[:, q * 128 : (q + 1) * 128]
-        fold[sub, :] = total
-        return 0
-
-    lax.fori_loop(0, 4, wb_part, 0)
-    total = fold[...]
-    hi = total.astype(BF16)
-    mid = (total - hi.astype(F32)).astype(BF16)
-    lo = (total - hi.astype(F32) - mid.astype(F32)).astype(BF16)
-    ones = jnp.ones((16, C), F32).astype(BF16)
-    bsum[0] = (nt(ones, hi) + nt(ones, mid) + nt(ones, lo))[0:8]
-    b1 = [copy(bsum.at[0], b1r.at[2 * a + b], B1 + 2 * a + b, peer(dx=a, ec=b)) for a, b in near]
-    begin(b1)
 
     def dpair_row(j, _):
         dbj = dball[j]
@@ -470,6 +519,7 @@
 
     end(ra4)
     end(rb4[1:])
+    pass_slab(3)
     for d in (1, 2, 3):
         dball[:, d, :] = r4[0, d].astype(F32) + r4[1, d].astype(F32)
     dball[:, 4:16, :] = jnp.zeros((OWN, 12, N), F32)
@@ -491,7 +541,7 @@
     o_dwout[...] = wtot[C : C + DH, :]
     slab_out = [pltpu.make_async_copy(dsl.at[i], o_dslab.at[i], load.at[i]) for i in range(ROWS)]
     for i in range(ROWS):
-        end(slab_copies(i))
+        end_slab(i)
         slab_out[i].start()
     end(b2)
     part = bsum[1]
@@ -539,11 +589,11 @@
         v((2, OWN, N), BF16),
         v((2, 4, OWN, N), BF16),
         v((OWN, OWN, N), F32),
-        v((ROWS, 2, 2, C, BLK), BF16),
-        v((ROWS, 2, C, BLK), BF16),
-        v((ROWS, C, BLK), BF16),
-        v((ROWS, C, BLK), BF16),
-        v((ROWS, 4, BLK, C), BF16),
+        v((ROWS, 2, C, HALF), BF16),
+        v((ROWS, 2, C, HALF), BF16),
+        v((ROWS, C, HALF), BF16),
+        v((ROWS, C, HALF), BF16),
+        v((ROWS, 2, HALF, C), BF16),
         v((OWN, DH, N), BF16),
         v((192, C), F32),
         v((8, 24, C), F32),
@@ -586,7 +636,7 @@
     vm = pl.BlockSpec(memory_space=pltpu.VMEM)
     anywhere = pl.BlockSpec(memory_space=pl.ANY)
     shapes = (
-        jax.ShapeDtypeStruct((ROWS, 4, BLK, C), BF16),
+        jax.ShapeDtypeStruct((ROWS, 2, HALF, C), BF16),
         jax.ShapeDtypeStruct((OWN, DH, N), BF16),
         jax.ShapeDtypeStruct((C, C), F32),
         jax.ShapeDtypeStruct((DH, C), F32),

time: 99.9 us -> 93.4 us (0.935)
  Pallas kernels: 98.8 us -> 92.4 us
    pallas_call x1, Pallas kernels: 96.2 us -> 89.7 us  [shards(): pl.pallas_call(kernel, out_shape=shapes, in_specs=[anywhere, anywhere, vm...]
where the time goes in v5:
time: 93.4 us; the launch traced here: 93.2 us
  Pallas kernels  92.4 us (99%)
    pallas_call x1, Pallas kernels, shards(): pl.pallas_call(kernel, out_shape=shapes, in_specs=[anywhere, anywhere, vm...  89.7 us
    pallas_call x1, Pallas kernels, shards(): pl.pallas_call(hand_on, out_shape=shapes, in_specs=[in_hbm] * 5, out_spec...  2.63 us

profile of v5, /device:TPU:1, one launch (start us, length us, event | category | flops | bytes accessed | tf_op | source)
XLA Modules:
  0.0 93.2 jit_solution(7553921068104358057)
XLA Ops:
  0.6 89.7 %shard_map.110 = (bf16[4,2,512,128]{3,2,1,0:T(8,128)(2,1)}, bf16[16,32,1024]{2,1,0:T(8,128)(2,1)}, f32[128,128]{1,0:T(8,128)}, f32[32,128]{1,0:T(8,128)}, f32[1,128]{1,0:T(1,128)}) custom-call(bf16[4,1024,128]{2,1,0:T(8,128)(2,1)} %slab_h.1, bf16[16,1024,128]{2,1,0:T(8,128)(2,1)} %pair_h.1, s32[4,1024]{1,0:T(4,128)} %mask.1, bf16[128,128]{1,0:T(8,128)(2,1)} %bitcast.10, ...), custom_call_target="tpu_custom_call" | custom-call | tf_op jit(solution)/shard_map/pallas_call | solution.py:645
  90.4 2.6 %shard_map.111 = (bf16[4,2,512,128]{3,2,1,0:T(8,128)(2,1)}, bf16[16,32,1024]{2,1,0:T(8,128)(2,1)}, f32[128,128]{1,0:T(8,128)}, f32[32,128]{1,0:T(8,128)}, f32[1,128]{1,0:T(1,128)}) custom-call(bf16[4,2,512,128]{3,2,1,0:T(8,128)(2,1)} %get-tuple-element.15.refs_0_, bf16[16,32,1024]{2,1,0:T(8,128)(2,1)} %get-tuple-element.16.refs_1_, ...), custom_call_target="tpu_custom_call" | custom-call | tf_op jit(solution)/shard_map/pallas_call | solution.py:656

commit v6 on v5

--- a/solution.py
+++ b/solution.py
@@ -50,7 +50,7 @@
 R1 = SEMS.take(2)
 R2 = SEMS.take(16)
 R3 = SEMS.take(16)
-R4 = SEMS.take(8)
+R4 = SEMS.take(4)
 S1 = SEMS.take(8)
 S2 = SEMS.take(4)
 T1 = SEMS.take(8)
@@ -114,7 +114,7 @@
     far = [(dy, ez) for dy in range(4) for ez in range(2) if dy or ez]
     peers = [peer(dx=a, ec=b) for a, b in near] + [peer(dy=a, ez=b) for a, b in far]
     for d in (1, 2, 3):
-        peers += [peer(dh=d), peer(ez=1, dh=d)]
+        peers.append(peer(dh=d))
     barrier = pltpu.get_barrier_semaphore()
     for to in peers:
         pl.semaphore_signal(barrier, inc=1, device_id=to, device_id_type=MESH)
@@ -231,11 +231,10 @@
     gac.start()
     gac.wait()
 
-    def block(i, yy, zs):
+    def block(i, zs):
         keep = mask[pl.ds(i, 1), :] == 1
-        two = pl.ds(2 * yy, 2)
-        zj = z[i, two, zs].reshape(BLK, C)
-        bias = plane[two, zs].reshape(BLK, N).astype(F32)
+        zj = z[i, :, zs].reshape(HALF, C)
+        bias = plane[:, zs].reshape(HALF, N).astype(F32)
         logits = nn(zj[:, 0:DH], rhs[i, 0:DH, 0:N]) * SCALE + bias
         logits = jnp.where(keep, logits, -1e9)
         expo = jnp.exp(logits - jnp.max(logits, axis=1, keepdims=True))
@@ -245,22 +244,14 @@
         dl = probs * (dp - jnp.sum(probs * dp, axis=1, keepdims=True))
         dl = jnp.where(keep, dl, 0.0)
         dlb = dl.astype(BF16)
-        dbias[two, zs] += dl.reshape(2, 4, 2, OWN, N)
+        dbias[:, zs] += dl.reshape(4, 4, 2, OWN, N)
         zall = z[i].reshape(N, C)
-        lane = lax.broadcasted_iota(jnp.int32, (BLK, C), 1)
+        lane = lax.broadcasted_iota(jnp.int32, (HALF, C), 1)
         nat = jnp.where(lane < 64, nn(dlb, zall), nn(pb, zall))
-        natt[i, two, zs] = nat.reshape(2, 128, C)
-        left = jnp.concatenate([zq[i, 4 * yy + zs], zq[i, 4 * yy + 2 + zs]], axis=1)
+        natt[i, :, zs] = nat.reshape(4, 128, C)
+        left = jnp.concatenate([zq[i, 2 * k + zs] for k in range(4)], axis=1)
         dkv[i, 0:DH, :] += nn(left[0:DH], dlb)
         dkv[i, DH:64, :] += nn(left[DH:64], pb)
-
-    def own_half(t, _):
-        block(t // 2, lax.rem(t, 2), zh)
-        return 0
-
-    def other_half(t, _):
-        block(t // 2, lax.rem(t, 2), oz)
-        return 0
 
     def up_copies(i):
         far_half = 1 - side
@@ -387,37 +378,28 @@
         for d in (1, 2, 3):
             low = low + r3a[s, d].astype(F32)
             high = high + r3b[s, d].astype(F32)
-        both = jnp.concatenate([low, high], axis=1)
-        s4[s] = both.astype(BF16)
-        out = []
-        for d in range(4):
-            if s or d:
-                out.append(copy(s4.at[s], r4.at[s, d], R4 + 4 * s + d, peer(ez=s, dh=d)))
-        return both, out
+        return jnp.concatenate([low, high], axis=1)
 
     def own_row(i):
-        lax.fori_loop(2 * i, 2 * i + 2, own_half, 0, unroll=2)
+        block(i, zh)
 
     def other_row(i):
-        lax.fori_loop(2 * i, 2 * i + 2, other_half, 0, unroll=2)
-
-    lax.fori_loop(0, 4, own_half, 0, unroll=2)
+        block(i, oz)
+
+    own_row(0)
+    own_row(1)
     end(gb2)
     gbc = gather_core(1)
     gbc.start()
+    own_row(2)
     gbc.wait()
-    for i in range(2):
+    for i in range(3):
         other_row(i)
         finish_row(i)
-    own_row(2)
-    middle_slab(0)
-    other_row(2)
-    finish_row(2)
-    middle_slab(1)
     own_row(3)
     ra1 = sum_core(0)
     ra1.start()
-    finish_slab(0)
+    middle_slab(0)
     other_row(3)
     rb1 = sum_core(1)
     rb1.start()
@@ -438,17 +420,17 @@
     rb2 = sum_first(1)
     begin(rb2)
     begin(w1)
-    finish_slab(1)
-    pass_slab(0)
-    middle_slab(2)
+    middle_slab(1)
+    finish_slab(0)
     ra1.wait()
     ra2 = sum_first(0)
     end(rb2)
     rb3 = sum_second(1)
     begin(rb3)
     begin(ra2)
-    pass_slab(1)
-    finish_slab(2)
+    middle_slab(2)
+    finish_slab(1)
+    pass_slab(0)
     end(w1)
     part = wacc[wslice(wid(0, 0)), :]
     for a, b in near:
@@ -456,21 +438,25 @@
     wpart[...] = part
     w2 = [copy(wpart, w2r.at[2 * a + b], W2 + 2 * a + b, peer(dy=a, ez=b)) for a, b in far]
     begin(w2)
+    end(rb3)
+    s4[1] = sum_last(1).astype(BF16)
+    rb4 = copy(s4.at[1], r4.at[0], R4, peer(ez=1))
+    rb4.start()
     middle_slab(3)
-    end(rb3)
-    _, rb4 = sum_last(1)
-    begin(rb4)
+    finish_slab(2)
+    pass_slab(1)
     end(ra2)
     ra3 = sum_second(0)
     begin(ra3)
-    pass_slab(2)
     finish_slab(3)
     end(ra3)
-    own, ra4 = sum_last(0)
-    begin(ra4)
-    rb4[0].wait()
-
-    db = own + r4[1, 0].astype(F32)
+    own = sum_last(0)
+    rb4.wait()
+
+    db = own + r4[0].astype(F32)
+    s4[0] = db.astype(BF16)
+    r5 = [copy(s4.at[0], r4.at[d], R4 + d, peer(dh=d)) for d in (1, 2, 3)]
+    begin(r5)
     own_bias[...] = db
     dball[:, 0, :] = db
 
@@ -494,6 +480,7 @@
     bsum[0] = (nt(ones, hi) + nt(ones, mid) + nt(ones, lo))[0:8]
     b1 = [copy(bsum.at[0], b1r.at[2 * a + b], B1 + 2 * a + b, peer(dx=a, ec=b)) for a, b in near]
     begin(b1)
+    pass_slab(2)
     end(w2)
     part = wpart[...]
     for a, b in far:
@@ -517,11 +504,9 @@
         dpair[j] = (rp[pl.ds(j, 1), :] * (g - first - yq[j] * second)).astype(BF16)
         return 0
 
-    end(ra4)
-    end(rb4[1:])
-    pass_slab(3)
+    end(r5)
     for d in (1, 2, 3):
-        dball[:, d, :] = r4[0, d].astype(F32) + r4[1, d].astype(F32)
+        dball[:, d, :] = r4[d].astype(F32)
     dball[:, 4:16, :] = jnp.zeros((OWN, 12, N), F32)
     lax.fori_loop(0, 8, dpair_row, 0, unroll=4)
     out_low = pltpu.make_async_copy(dpair.at[0:8], o_dpair.at[0:8], load.at[4])
@@ -533,6 +518,7 @@
     bsum[1] = part
     b2 = [copy(bsum.at[1], b2r.at[2 * a + b], B2 + 2 * a + b, peer(dy=a, ez=b)) for a, b in far]
     begin(b2)
+    pass_slab(3)
     lax.fori_loop(8, OWN, dpair_row, 0, unroll=4)
     out_high = pltpu.make_async_copy(dpair.at[8:16], o_dpair.at[8:16], load.at[5])
     out_high.start()
@@ -587,7 +573,7 @@
         v((2, 4, OWN, HALF), BF16),
         v((2, 4, OWN, HALF), BF16),
         v((2, OWN, N), BF16),
-        v((2, 4, OWN, N), BF16),
+        v((4, OWN, N), BF16),
         v((OWN, OWN, N), F32),
         v((ROWS, 2, C, HALF), BF16),
         v((ROWS, 2, C, HALF), BF16),

time: 93.4 us -> 88.8 us (0.951)
  Pallas kernels: 92.4 us -> 87 us
    pallas_call x1, Pallas kernels: 89.7 us -> 84.4 us  [shards(): pl.pallas_call(kernel, out_shape=shapes, in_specs=[anywhere, anywhere, vm...]
where the time goes in v6:
time: 88.8 us; the launch traced here: 87.8 us
  Pallas kernels  87 us (98%)
    pallas_call x1, Pallas kernels, shards(): pl.pallas_call(kernel, out_shape=shapes, in_specs=[anywhere, anywhere, vm...  84.4 us
    pallas_call x1, Pallas kernels, shards(): pl.pallas_call(hand_on, out_shape=shapes, in_specs=[in_hbm] * 5, out_spec...  2.63 us

profile of v6, /device:TPU:1, one launch (start us, length us, event | category | flops | bytes accessed | tf_op | source)
XLA Modules:
  0.0 87.8 jit_solution(11439033654895586271)
XLA Ops:
  0.6 84.4 %shard_map.110 = (bf16[4,2,512,128]{3,2,1,0:T(8,128)(2,1)}, bf16[16,32,1024]{2,1,0:T(8,128)(2,1)}, f32[128,128]{1,0:T(8,128)}, f32[32,128]{1,0:T(8,128)}, f32[1,128]{1,0:T(1,128)}) custom-call(bf16[4,1024,128]{2,1,0:T(8,128)(2,1)} %slab_h.1, bf16[16,1024,128]{2,1,0:T(8,128)(2,1)} %pair_h.1, s32[4,1024]{1,0:T(4,128)} %mask.1, bf16[128,128]{1,0:T(8,128)(2,1)} %bitcast.10, ...), custom_call_target="tpu_custom_call" | custom-call | tf_op jit(solution)/shard_map/pallas_call | solution.py:631
  85.0 2.6 %shard_map.111 = (bf16[4,2,512,128]{3,2,1,0:T(8,128)(2,1)}, bf16[16,32,1024]{2,1,0:T(8,128)(2,1)}, f32[128,128]{1,0:T(8,128)}, f32[32,128]{1,0:T(8,128)}, f32[1,128]{1,0:T(1,128)}) custom-call(bf16[4,2,512,128]{3,2,1,0:T(8,128)(2,1)} %get-tuple-element.15.refs_0_, bf16[16,32,1024]{2,1,0:T(8,128)(2,1)} %get-tuple-element.16.refs_1_, ...), custom_call_target="tpu_custom_call" | custom-call | tf_op jit(solution)/shard_map/pallas_call | solution.py:642

commit v7 on v6

--- a/solution.py
+++ b/solution.py
@@ -448,7 +448,6 @@
     end(ra2)
     ra3 = sum_second(0)
     begin(ra3)
-    finish_slab(3)
     end(ra3)
     own = sum_last(0)
     rb4.wait()
@@ -480,6 +479,7 @@
     bsum[0] = (nt(ones, hi) + nt(ones, mid) + nt(ones, lo))[0:8]
     b1 = [copy(bsum.at[0], b1r.at[2 * a + b], B1 + 2 * a + b, peer(dx=a, ec=b)) for a, b in near]
     begin(b1)
+    finish_slab(3)
     pass_slab(2)
     end(w2)
     part = wpart[...]

time: 88.8 us -> 88.7 us (level)
  no operation moved by 1% of the time
where the time goes in v7:
time: 88.7 us; the launch traced here: 88.1 us
  Pallas kernels  87.3 us (98%)
    pallas_call x1, Pallas kernels, shards(): pl.pallas_call(kernel, out_shape=shapes, in_specs=[anywhere, anywhere, vm...  84.6 us
    pallas_call x1, Pallas kernels, shards(): pl.pallas_call(hand_on, out_shape=shapes, in_specs=[in_hbm] * 5, out_spec...  2.63 us

profile of v7, /device:TPU:1, one launch (start us, length us, event | category | flops | bytes accessed | tf_op | source)
XLA Modules:
  0.0 88.1 jit_solution(8091119838079960288)
XLA Ops:
  0.6 84.6 %shard_map.110 = (bf16[4,2,512,128]{3,2,1,0:T(8,128)(2,1)}, bf16[16,32,1024]{2,1,0:T(8,128)(2,1)}, f32[128,128]{1,0:T(8,128)}, f32[32,128]{1,0:T(8,128)}, f32[1,128]{1,0:T(1,128)}) custom-call(bf16[4,1024,128]{2,1,0:T(8,128)(2,1)} %slab_h.1, bf16[16,1024,128]{2,1,0:T(8,128)(2,1)} %pair_h.1, s32[4,1024]{1,0:T(4,128)} %mask.1, bf16[128,128]{1,0:T(8,128)(2,1)} %bitcast.10, ...), custom_call_target="tpu_custom_call" | custom-call | tf_op jit(solution)/shard_map/pallas_call | solution.py:631
  85.3 2.6 %shard_map.111 = (bf16[4,2,512,128]{3,2,1,0:T(8,128)(2,1)}, bf16[16,32,1024]{2,1,0:T(8,128)(2,1)}, f32[128,128]{1,0:T(8,128)}, f32[32,128]{1,0:T(8,128)}, f32[1,128]{1,0:T(1,128)}) custom-call(bf16[4,2,512,128]{3,2,1,0:T(8,128)(2,1)} %get-tuple-element.15.refs_0_, bf16[16,32,1024]{2,1,0:T(8,128)(2,1)} %get-tuple-element.16.refs_1_, ...), custom_call_target="tpu_custom_call" | custom-call | tf_op jit(solution)/shard_map/pallas_call | solution.py:642
